TPU v7x, 128 devices: a whole 4x4x4 slice. The times are simulated.
128 devices in a mesh: dp: 8 (over x, core), tensor: 16 (over z, y).
Axes of the slice: x: 4, y: 4, z: 4, core: 2. Of those that a mesh axis runs over, the one named last changes fastest.
Arguments:
- hidden_acts: bfloat16 [16384, 14336], P('dp', 'tensor'), may hold values from -6 to 6
- cotangent: bfloat16 [16384, 4096], P(('dp', 'tensor')), may hold values from -0.125 to 0.125
- error_buffer: bfloat16 [8, 4096, 14336], P('dp', None, 'tensor'), may hold values from -6 to 6
- q_start: float32 [14336, 32], P('tensor'), may hold values from -0.046875 to 0.046875
Outputs:
- new_error: bfloat16 [8, 4096, 14336], P('dp', None, 'tensor')
- q_mean: float32 [14336, 32], P('tensor')
All inputs are finite; a program needn't handle non-finite values.
Results may differ from a plain program's by a relative error of at most 0.00045.
Values may be sent and summed in bfloat16 or wider, within the bound.
No kernel may reach another device: no remote copies, remote signals or barrier semaphores. Data moves between devices by JAX's collectives and lax.ppermute only.
A program may use at most 128 MiB of HBM per device.

v0:
```python
import jax
import jax.numpy as jnp
from jax import lax
from jax.sharding import PartitionSpec as P


def on_device(hidden_acts, cotangent, error_buffer, q_start):
    highest = lax.Precision.HIGHEST
    gradient = lax.dot_general(
        lax.all_gather(cotangent, "tensor", axis=0, tiled=True),
        hidden_acts,
        (((0,), (0,)), ((), ())),
        preferred_element_type=jnp.float32,
    )
    merged = gradient + error_buffer[0].astype(jnp.float32)
    local_power = jnp.dot(merged, q_start, precision=highest)
    power = lax.psum(local_power, ("dp", "tensor"))
    gram_matrix = jnp.dot(power.T, power, precision=highest)
    factor_lower = jnp.linalg.cholesky(gram_matrix)
    basis = jax.scipy.linalg.solve_triangular(factor_lower, power.T, lower=True).T
    q_local = lax.dot_general(merged, basis, (((0,), (0,)), ((), ())), precision=highest)
    q_mean = lax.psum(q_local, "dp") / lax.axis_size("dp")
    update = jnp.dot(basis, q_mean.T, precision=highest)
    new_error = (merged - update).astype(jnp.bfloat16)
    return (new_error[None], q_mean)


def solution(mesh):
    placed = (
        P("dp", "tensor"),
        P(("dp", "tensor"), None),
        P("dp", None, "tensor"),
        P("tensor", None),
    )
    return jax.shard_map(
        on_device,
        mesh=mesh,
        in_specs=placed,
        out_specs=(P("dp", None, "tensor"), P("tensor", None)),
        check_vma=False,
    )
```

profile of v0, /device:TPU:1, one launch (start us, length us, event | category | flops | bytes accessed | tf_op | source)
XLA Modules:
  0.0 413.6 jit_solution(12871225892543970121)
XLA Ops:
  7.2 0.0 copy-start
  7.2 0.0 all-gather.2.cloned.1.call-start
  7.2 0.7 all-gather.2.cloned.1.call-update
  7.9 0.0 all-reduce.3.cloned.1.call-start
  8.0 116.9 %all-gather.2.cloned.1.call-done = bf16[2048,4096]{1,0:T(8,128)(2,1)} async-done(((bf16[128,4096]{1,0:T(8,128)(2,1)}), bf16[2048,4096]{1,0:T(8,128)(2,1)}) %all-gather.2.cloned.1.call-update) | async-done | bytes 16777232 | tf_op jit(solution)/shard_map/all_gather | solution.py:10
  124.8 23.2 %convert_add_fusion = f32[4096,896]{1,0:T(8,128)S(1)} fusion(bf16[2048,4096]{1,0:T(8,128)(2,1)} %all-gather.2.cloned.1.call-done, bf16[2048,896]{1,0:T(8,128)(2,1)} %param.4, bf16[1,4096,896]{2,1,0:T(8,128)(2,1)} %param.6), kind=kOutput, calls=%fused_computation | convolution fusion | flops 15039725568 | bytes 42467328 | tf_op jit(solution)/shard_map/dot_general | solution.py:9
  148.0 0.0 copy-start.1
  148.0 5.2 %copy-done.1 = f32[4096,896]{1,0:T(8,128)} copy-done((f32[4096,896]{1,0:T(8,128)}, f32[4096,896]{1,0:T(8,128)S(1)}, u32[]{:S(2)}) %copy-start.1) | copy-done | bytes 14680088
  153.2 0.0 copy-done
  153.2 14.5 %fusion.5 = f32[4096,32]{0,1:T(8,128)} fusion(f32[4096,896]{1,0:T(8,128)S(1)} %convert_add_fusion, f32[896,32]{0,1:T(8,128)S(1)} %copy-done), kind=kOutput, calls=%fused_computation.14 | convolution fusion | flops 1409286144 | bytes 15319040 | tf_op jit(solution)/shard_map/dot_general | solution.py:16
  167.7 0.0 all-reduce.3.cloned.1.call-update
  167.7 0.3 all-reduce.5.cloned.1.call-start
  168.0 144.7 %all-reduce.3.cloned.1.call-done = f32[4096,32]{0,1:T(8,128)} async-done(((f32[4096,32]{0,1:T(8,128)}), f32[4096,32]{0,1:T(8,128)}) %all-reduce.3.cloned.1.call-update) | async-done | bytes 524304 | tf_op jit(solution)/shard_map/psum | solution.py:17
  312.8 1.8 fusion.6
  314.5 0.1 copy.6
  314.6 2.9 cholesky.16
  317.6 0.6 compare_reduce_fusion
  318.2 0.7 fusion.1
  318.9 2.4 custom-call.7
  321.3 1.7 fusion.2
  323.0 11.9 %fusion.7 = f32[896,32]{0,1:T(8,128)} fusion(f32[4096,896]{1,0:T(8,128)} %copy-done.1, f32[32,4096]{1,0:T(8,128)S(1)} %fusion.2), kind=kOutput, calls=%fused_computation.16 | convolution fusion | flops 1409286144 | bytes 15319040 | tf_op jit(solution)/shard_map/dot_general | solution.py:21
  334.8 0.0 all-reduce.5.cloned.1.call-update
  334.9 55.5 %all-reduce.5.cloned.1.call-done = f32[896,32]{0,1:T(8,128)} async-done(((f32[896,32]{0,1:T(8,128)}), f32[896,32]{0,1:T(8,128)}) %all-reduce.5.cloned.1.call-update) | async-done | bytes 114704 | tf_op jit(solution)/shard_map/psum | solution.py:22
  390.4 0.9 broadcast_multiply_fusion
  391.3 0.0 copy-start.2
  391.3 15.7 %fusion = bf16[1,4096,896]{2,1,0:T(8,128)(2,1)} fusion(f32[4096,896]{1,0:T(8,128)} %copy-done.1, f32[32,4096]{1,0:T(8,128)S(1)} %fusion.2, f32[896,32]{0,1:T(8,128)S(1)} %broadcast_multiply_fusion), kind=kOutput, calls=%fused_computation.2 | convolution fusion | flops 1416626176 | bytes 22659072 | tf_op jit(solution)/shard_map/dot_general | solution.py:23
  407.1 0.0 copy-done.2
  (2 shorter events, 0.0 us)
Async XLA Ops:
  7.2 146.1 %copy-start = (f32[896,32]{0,1:T(8,128)S(1)}, f32[896,32]{0,1:T(8,128)}, u32[]{:S(2)}) copy-start(f32[896,32]{0,1:T(8,128)} %param.7) | copy-start | bytes 344068
  7.2 117.7 %all-gather.2.cloned.1.call-start = ((), (), s32[]{:S(2)}) async-start(), calls=%async_computation | async-start | bytes 17825792 | tf_op jit(solution)/shard_map/all_gather | solution.py:10
  7.9 304.8 %all-reduce.3.cloned.1.call-start = ((), (), s32[]{:S(2)}) async-start(), calls=%async_computation.1 | async-start | bytes 1048576 | tf_op jit(solution)/shard_map/psum | solution.py:17
  148.0 5.2 %copy-start.1 = (f32[4096,896]{1,0:T(8,128)}, f32[4096,896]{1,0:T(8,128)S(1)}, u32[]{:S(2)}) copy-start(f32[4096,896]{1,0:T(8,128)S(1)} %convert_add_fusion) | copy-start | bytes 44040196
  167.7 222.7 %all-reduce.5.cloned.1.call-start = ((), (), s32[]{:S(2)}) async-start(), calls=%async_computation.2 | async-start | bytes 229376 | tf_op jit(solution)/shard_map/psum | solution.py:22
  391.3 15.8 %copy-start.2 = (f32[896,32]{0,1:T(8,128)}, f32[896,32]{0,1:T(8,128)S(1)}, u32[]{:S(2)}) copy-start(f32[896,32]{0,1:T(8,128)S(1)} %broadcast_multiply_fusion) | copy-start | bytes 344068
Sparse Core Ops, SparseCore 0:
  10.2 114.6 all-gather.1
  167.9 144.8 all-reduce.2
  335.0 55.3 all-reduce.4
where the time goes:
time: 414 us
  waiting for transfers between devices  318 us (77%)
  matrix products  68.7 us (17%)
  between operations  13.8 us (3%)
  other arithmetic  7.6 us (2%)
  local copies, waits for them, and re-layouts  5.29 us (1%)
    psum x1, waiting for transfers between devices, on_device(): power = lax.psum(local_power, ('dp', 'tensor'))  145 us
    all_gather x1, waiting for transfers between devices, on_device(): lax.all_gather(cotangent, 'tensor', axis=0, tiled=True)  117 us
    psum x1, waiting for transfers between devices, on_device(): q_mean = lax.psum(q_local, 'dp') / lax.axis_size('dp')  55.5 us
    dot_general x1, matrix products, on_device(): lax.dot_general(lax.all_gather(cotangent, 'tensor', axis=0, tiled=True),...  23.2 us
    dot_general x1, matrix products, on_device(): update = jnp.dot(basis, q_mean.T, precision=highest)  15.7 us
    dot_general x1, matrix products, on_device(): local_power = jnp.dot(merged, q_start, precision=highest)  14.5 us
    dot_general x1, matrix products, on_device(): lax.dot_general(merged, basis, (((0,), (0,)), ((), ())), precision=highest)  11.9 us
  transfers between devices with their start and end apart: 3, of which 3 were waited for; matrix products, arithmetic and copies ran while one was open for 0% of the time, Pallas kernels for 0%

commit v1 on v0

v1 whole, which is shorter than its diff:
```python
import jax
import jax.numpy as jnp
from jax import lax
from jax.experimental import pallas as pl
from jax.experimental.pallas import tpu as pltpu
from jax.sharding import PartitionSpec as P

AXES = ("dp", "tensor")
RANK = 32
NX, NC, NZ, NY = 4, 2, 4, 4
N_DP = NX * NC
TOK = 128
TILE = 128
BLOCK = 512
F32, BF16 = jnp.float32, jnp.bfloat16
SMEM = pl.BlockSpec(memory_space=pltpu.SMEM)


def receive_from(x=0, c=0, z=0, y=0):
    pairs = []
    for ix in range(NX):
        for ic in range(NC):
            for iz in range(NZ):
                for iy in range(NY):
                    target = ((ix * NC + ic) * NZ + iz) * NY + iy
                    source = (((ix + x) % NX * NC + (ic + c) % NC) * NZ + (iz + z) % NZ) * NY + (iy + y) % NY
                    pairs.append((source, target))
    return pairs


def fetch(array, **offsets):
    return lax.ppermute(array, AXES, receive_from(**offsets))


def around(arrays, axis):
    return [arrays[0]] + [fetch(arrays[k], **{axis: k}) for k in (1, 2, 3)]


def f32(*shape):
    return jax.ShapeDtypeStruct(shape, F32)


def bf16(*shape):
    return jax.ShapeDtypeStruct(shape, BF16)


def whole(array):
    zeros = (0,) * len(array.shape)
    return pl.BlockSpec(tuple(array.shape), lambda *_: zeros)


def kernel_call(body, grid, operands, in_specs, outs, out_specs, scratch=(), aliases=None, vmem_mib=24, after=()):
    count = len(operands)
    operands = [*operands, *after]
    in_specs = [*in_specs, *[pl.BlockSpec(memory_space=pltpu.HBM)] * len(after)]

    def call(*refs):
        body(*refs[:count], *refs[count + len(after):])

    return pl.pallas_call(
        call,
        grid=(grid,),
        in_specs=[whole(a) if s is None else s for a, s in zip(operands, in_specs)],
        out_specs=[whole(a) if s is None else s for a, s in zip(outs, out_specs)],
        out_shape=outs,
        scratch_shapes=list(scratch),
        input_output_aliases=aliases or {},
        compiler_params=pltpu.CompilerParams(vmem_limit_bytes=vmem_mib * 2 ** 20),
        cost_estimate=pl.CostEstimate(flops=2 ** 20, bytes_accessed=2 ** 16, transcendentals=0),
    )(*operands)


def split3(value):
    high = value.astype(BF16)
    rest = value - high.astype(F32)
    middle = rest.astype(BF16)
    low = (rest - middle.astype(F32)).astype(BF16)
    return jnp.concatenate([high, middle, low], axis=0)


def fold3(product):
    return product[:RANK] + (product[RANK:2 * RANK] + product[2 * RANK:])


def dot_nt(a, b):
    return lax.dot_general(a, b, (((1,), (1,)), ((), ())), preferred_element_type=F32)


def dot_nn(a, b):
    return jnp.dot(a, b, preferred_element_type=F32)


def hq_body(q_t, h, out, pieces):
    @pl.when(pl.program_id(0) == 0)
    def _():
        pieces[...] = split3(q_t[...])

    part = fold3(dot_nt(pieces[...], h[...]))
    for y in range(NY):
        out[y] = part[:, y * TOK:(y + 1) * TOK]


def eq_body(q_t, e, out, pieces):
    @pl.when(pl.program_id(0) == 0)
    def _():
        pieces[...] = split3(q_t[...])

    out[...] = fold3(dot_nt(pieces[...], e[...]))


def power_body(hq, ct, eq, out, lhs):
    @pl.when(pl.program_id(0) == 0)
    def _():
        total = hq[0]
        for t in range(1, NZ * NY):
            total += hq[t]
        lhs[...] = split3(total)

    term = fold3(dot_nt(lhs[...], ct[...])) + eq[...]
    for j in range(BLOCK // TILE):
        for i in range(RANK // 8):
            out[j * (RANK // 8) + i] = term[i * 8:(i + 1) * 8, j * TILE:(j + 1) * TILE]


def tile_sum_body(tiles, out):
    totals = [tiles[k] for k in range(4)]
    for k in range(4, tiles.shape[0]):
        totals[k % 4] += tiles[k]
    out[...] = jnp.broadcast_to(((totals[0] + totals[1]) + (totals[2] + totals[3]))[None], out.shape)


def cp_body(tiles, ct, power, pieces, out, acc):
    i = pl.program_id(0)

    @pl.when(i == 0)
    def _():
        acc[...] = jnp.zeros_like(acc)

    n = RANK // 8
    block = jnp.concatenate([
        jnp.concatenate([tiles[j * n + k] for k in range(n)], axis=0) for j in range(BLOCK // TILE)
    ], axis=1)
    power[...] = block
    split = split3(block)
    pieces[...] = split
    acc[...] += fold3(dot_nn(split, ct[...]))

    @pl.when(i == pl.num_programs(0) - 1)
    def _():
        out[...] = jnp.broadcast_to(acc[...][None], out.shape)


def basis_body(power, pieces, e, ep, inverse, basis, acc, gram):
    i = pl.program_id(0)

    @pl.when(i == 0)
    def _():
        acc[...] = jnp.zeros_like(acc)
        gram[...] = lax.dot_general(
            power[...], power[...], (((1,), (1,)), ((), ())), precision=lax.Precision.HIGHEST, preferred_element_type=F32
        )

    acc[...] += fold3(dot_nn(pieces[...], e[...]))

    @pl.when(i == pl.num_programs(0) - 1)
    def _():
        ep[...] = acc[...]
        row = lax.broadcasted_iota(jnp.int32, (RANK, 2 * RANK), 0)
        column = lax.broadcasted_iota(jnp.int32, (RANK, 2 * RANK), 1)
        work = jnp.concatenate([gram[...], jnp.zeros((RANK, RANK), F32)], axis=1)
        work = jnp.where(column == row + RANK, 1.0, work)
        for j in range(RANK):
            factor = work[:, j:j + 1] / work[j:j + 1, j:j + 1]
            work = work - jnp.where(row > j, factor, 0.0) * work[j:j + 1, :]
        pivots = jnp.sum(jnp.where(column == row, work, 0.0), axis=1, keepdims=True)
        inv = work[:, RANK:] / jnp.sqrt(pivots)
        inverse[...] = inv
        b = jnp.dot(inv, power[...], precision=lax.Precision.HIGHEST, preferred_element_type=F32)
        b = split3(b)
        high, middle, low = b[:RANK], b[RANK:2 * RANK], b[2 * RANK:]
        basis[...] = jnp.concatenate([high, high, middle, high, low, middle], axis=0)


def q_body(cp, h, ep, out, acc):
    i = pl.program_id(0)

    @pl.when(i == 0)
    def _():
        acc[...] = ep[...]

    left = split3(jnp.concatenate([cp[y] for y in range(NY)], axis=1))
    acc[...] += fold3(dot_nn(left, h[...]))

    @pl.when(i == NZ - 1)
    def _():
        out[...] = acc[...]


def mean_body(inverse, p0, p1, p2, p3, q_mean, pieces):
    total = (p0[...] + p1[...]) + (p2[...] + p3[...])
    mean = jnp.dot(inverse[...], total, precision=lax.Precision.HIGHEST, preferred_element_type=F32) * (1.0 / N_DP)
    q_mean[...] = mean
    s = split3(mean)
    high, middle, low = s[:RANK], s[RANK:2 * RANK], s[2 * RANK:]
    pieces[...] = jnp.concatenate([high, middle, high, low, high, middle], axis=0)


def error_body(g, h, basis, q, e, out):
    left = jnp.concatenate([g[t] for t in range(NZ * NY)], axis=1)
    acc = dot_nn(left, h[...])
    update = lax.dot_general(basis[...], q[...], (((0,), (0,)), ((), ())), preferred_element_type=F32)
    out[...] = ((acc + e[...].astype(F32)) - update).astype(BF16)


def error_call(gathered, h, basis, q, e):
    rows, columns = e.shape
    in_rows = pl.BlockSpec((BLOCK, columns), lambda i: (i, 0))
    return kernel_call(
        error_body, rows // BLOCK, [gathered, h, basis, q, e],
        [pl.BlockSpec((NZ * NY, BLOCK, TOK), lambda i: (0, i, 0)), None,
         pl.BlockSpec((basis.shape[0], BLOCK), lambda i: (0, i)), None, in_rows],
        [bf16(rows, columns)], [in_rows], vmem_mib=40,
    )[0]


def on_device(hidden, cotangent, error, q_start):
    error = error[0]
    rows = cotangent.shape[1]
    columns = hidden.shape[1]
    n_blocks = rows // BLOCK

    ct = cotangent.T
    gathered = lax.all_gather(ct, "tensor", axis=0)

    q_t = q_start.T
    (hq,) = kernel_call(
        hq_body, NZ, [q_t, hidden], [None, pl.BlockSpec((4 * TOK, columns), lambda i: (i, 0))],
        [f32(NZ * NY, RANK, TOK)], [pl.BlockSpec((NY, RANK, TOK), lambda i: (i, 0, 0))],
        scratch=[pltpu.VMEM((3 * RANK, columns), BF16)],
    )
    hq = lax.all_to_all(hq, "tensor", 0, 0)
    row_spec = pl.BlockSpec((BLOCK, columns), lambda i: (i, 0))
    column_spec = pl.BlockSpec((RANK, BLOCK), lambda i: (0, i))
    (eq,) = kernel_call(
        eq_body, n_blocks, [q_t, error], [None, row_spec], [f32(RANK, rows)], [column_spec],
        scratch=[pltpu.VMEM((3 * RANK, columns), BF16)],
    )
    stack_specs = [
        pl.BlockSpec((BLOCK, 4 * TOK), lambda i, n=n: (jnp.clip(i - 2 * n, 0, 1), 0)) for n in range(4)
    ]
    ct_spec = pl.BlockSpec((BLOCK, TOK), lambda i: (i, 0))
    n_tiles = RANK // 8 * (rows // TILE)
    tile_spec = pl.BlockSpec((n_tiles // n_blocks, 8, TILE), lambda i: (i, 0, 0))
    (tiles,) = kernel_call(
        power_body, n_blocks, [hq, ct, eq], [None, ct_spec, column_spec], [f32(n_tiles, 8, TILE)], [tile_spec],
        scratch=[pltpu.VMEM((3 * RANK, TOK), BF16)],
    )
    tiles = lax.all_to_all(tiles, AXES, 0, 0)
    (tiles,) = kernel_call(tile_sum_body, 1, [tiles], [None], [f32(n_tiles, 8, TILE)], [None])
    tiles = lax.all_to_all(tiles, AXES, 0, 0)
    power, pieces, cp = kernel_call(
        cp_body, n_blocks, [tiles, ct], [tile_spec, ct_spec],
        [f32(RANK, rows), bf16(3 * RANK, rows), f32(NZ * NY, RANK, TOK)],
        [column_spec, pl.BlockSpec((3 * RANK, BLOCK), lambda i: (0, i)), None],
        scratch=[pltpu.VMEM((RANK, TOK), F32)],
    )
    cp = lax.all_to_all(cp, "tensor", 0, 0)
    ep, inverse, basis = kernel_call(
        basis_body, n_blocks, [power, pieces, error],
        [None, pl.BlockSpec((3 * RANK, BLOCK), lambda i: (0, i)), row_spec],
        [f32(RANK, columns), f32(RANK, RANK), bf16(6 * RANK, rows)], [None] * 3,
        scratch=[pltpu.VMEM((RANK, columns), F32), pltpu.VMEM((RANK, RANK), F32)],
    )
    (q_raw,) = kernel_call(
        q_body, NZ, [cp, hidden, ep],
        [pl.BlockSpec((NY, RANK, TOK), lambda i: (i, 0, 0)), pl.BlockSpec((4 * TOK, columns), lambda i: (i, 0)), None],
        [f32(RANK, columns)], [None], scratch=[pltpu.VMEM((RANK, columns), F32)],
    )
    q_raw = q_raw + fetch(q_raw, c=1)
    q_mean, q_pieces = kernel_call(
        mean_body, 1, [inverse, *around([q_raw] * 4, "x")], [None] * 5,
        [f32(RANK, columns), bf16(6 * RANK, columns)], [None] * 2,
    )

    out = error_call(gathered, hidden, basis, q_pieces, error)
    return out[None], q_mean.T


def solution(mesh):
    placed = (
        P("dp", "tensor"),
        P(("dp", "tensor"), None),
        P("dp", None, "tensor"),
        P("tensor", None),
    )
    return jax.shard_map(
        on_device,
        mesh=mesh,
        in_specs=placed,
        out_specs=(P("dp", None, "tensor"), P("tensor", None)),
        check_vma=False,
    )
```

time: 414 us -> 177 us (0.43)
  waiting for transfers between devices: 318 us -> 42.3 us
  matrix products: 68.7 us -> 0 us
  Pallas kernels: 0 us -> 42.2 us
  blocking collectives: 0 us -> 40.4 us
  starting transfers between devices: 0.34 us -> 18 us
  local copies, waits for them, and re-layouts: 5.29 us -> 19.5 us
  other arithmetic: 7.6 us -> 0.01 us
    psum x2 -> x0, waiting for transfers between devices: 200 us -> none  [the longest x1 145 us: on_device(): power = lax.psum(local_power, ('dp', 'tensor'))]
    all_gather x1, waiting for transfers between devices: 117 us -> 33.6 us  [on_device(): gathered = lax.all_gather(ct, 'tensor', axis=0)]
    dot_general x5 -> x0, matrix products: 67 us -> none  [the longest x1 23.2 us: on_device(): lax.dot_general(lax.all_gather(cotangent, 'tensor', axis=0, tiled=True),...]
    pallas_call x0 -> x9, Pallas kernels: none -> 42.2 us  [kernel_call(): pl.pallas_call(call, grid=(grid,), in_specs=[whole(a) if s is None else s...]
    all_to_all x0 -> x2, blocking collectives: none -> 40.4 us  [on_device(): tiles = lax.all_to_all(tiles, AXES, 0, 0)]
    unnamed x6 -> x19, local copies, waits for them, and re-layouts: 5.22 us -> 19.5 us
    all_to_all x0 -> x2, starting transfers between devices: none -> 12.1 us  [the longest x1 8.59 us: on_device(): hq = lax.all_to_all(hq, 'tensor', 0, 0)]
    another operation x5 -> x0, other arithmetic: 6.68 us -> none  [the longest x3 3.6 us: on_device(): factor_lower = jnp.linalg.cholesky(gram_matrix)]
  transfers between devices with their start and end apart: 3 -> 7, of which waited for: 3 -> 7; matrix products, arithmetic and copies ran while one was open for 0% -> 0% of each run, Pallas kernels for 0% -> 10%
where the time goes in v1:
time: 177 us; the launch traced here: 176 us
  waiting for transfers between devices  42.3 us (24%)
  Pallas kernels  42.2 us (24%)
  blocking collectives  40.4 us (23%)
  local copies, waits for them, and re-layouts  19.5 us (11%)
  starting transfers between devices  18 us (10%)
  between operations  14.1 us (8%)
    pallas_call x9, Pallas kernels, kernel_call(): pl.pallas_call(call, grid=(grid,), in_specs=[whole(a) if s is None else s...  42.2 us
    all_to_all x2, blocking collectives, on_device(): tiles = lax.all_to_all(tiles, AXES, 0, 0)  40.4 us
    all_gather x1, waiting for transfers between devices, on_device(): gathered = lax.all_gather(ct, 'tensor', axis=0)  33.6 us
    unnamed x19, local copies, waits for them, and re-layouts  19.5 us
    all_to_all x1, starting transfers between devices, on_device(): hq = lax.all_to_all(hq, 'tensor', 0, 0)  8.59 us
    ppermute x4, starting transfers between devices, fetch(): return lax.ppermute(array, AXES, receive_from(**offsets))  5.79 us
    ppermute x4, waiting for transfers between devices, fetch(): return lax.ppermute(array, AXES, receive_from(**offsets))  5.39 us
  transfers between devices with their start and end apart: 7, of which 7 were waited for; matrix products, arithmetic and copies ran while one was open for 0% of the time, Pallas kernels for 10%

profile of v1, /device:TPU:1, one launch (start us, length us, event | category | flops | bytes accessed | tf_op | source)
XLA Modules:
  0.0 176.5 jit_solution(14977906658525844565)
XLA Ops:
  7.2 0.0 copy-start.8
  7.2 0.0 all-gather.3.cloned.1.call-start
  7.2 2.3 %copy.6 = bf16[128,4096]{0,1:T(8,128)(2,1)} copy(bf16[128,4096]{1,0:T(8,128)(2,1)} %param.5) | data formatting | bytes 2097152 | tf_op args[1]
  9.5 0.0 copy-start.6
  9.5 0.0 all-gather.3.cloned.1.call-update
  9.5 0.0 copy-start.3
  9.5 2.1 %copy-done.3 = bf16[2048,896]{1,0:T(8,128)(2,1)S(1)} copy-done((bf16[2048,896]{1,0:T(8,128)(2,1)S(1)}, bf16[2048,896]{1,0:T(8,128)(2,1)}, u32[]{:S(2)}) %copy-start.3) | copy-done | bytes 3670040
  11.6 0.0 copy-start.7
  11.6 0.9 copy-done.7
  12.5 2.5 %shard_map.59 = f32[16,32,128]{2,1,0:T(8,128)} custom-call(f32[32,896]{1,0:T(8,128)S(1)} %bitcast.12, bf16[2048,896]{1,0:T(8,128)(2,1)S(1)} %copy-done.3), custom_call_target="tpu_custom_call" | custom-call | flops 1048576 | bytes 65536 | tf_op jit(solution)/shard_map/pallas_call | solution.py:60
  15.0 8.6 %all-to-all-start = ((f32[16,32,128]{2,1,0:T(8,128)}), f32[16,32,128]{2,1,0:T(8,128)S(1)}, u32[]{:S(2)}, u32[]{:S(2)}) async-start(f32[16,32,128]{2,1,0:T(8,128)} %shard_map.59), calls=%async_computation | async-start | bytes 524288 | tf_op jit(solution)/shard_map/all_to_all | solution.py:241
  23.6 0.0 copy-done.8
  23.7 0.0 copy-start
  23.7 3.8 %copy-done = bf16[1,4096,896]{2,1,0:T(8,128)(2,1)S(1)} copy-done((bf16[1,4096,896]{2,1,0:T(8,128)(2,1)S(1)}, bf16[1,4096,896]{2,1,0:T(8,128)(2,1)}, u32[]{:S(2)}) %copy-start) | copy-done | bytes 7340056
  27.5 3.4 %shard_map.60.refs_2_ = f32[32,4096]{1,0:T(8,128)S(1)} custom-call(f32[32,896]{1,0:T(8,128)S(1)} %bitcast.13, bf16[4096,896]{1,0:T(8,128)(2,1)S(1)} %bitcast.6), custom_call_target="tpu_custom_call" | custom-call | flops 1048576 | bytes 65536 | tf_op jit(solution)/shard_map/pallas_call | solution.py:60
  30.9 1.5 all-to-all-done.refs_0_
  32.4 0.0 copy-done.6
  32.4 1.6 shard_map.61
  34.0 22.3 %all_to_all.20.refs_0_ = f32[128,8,128]{2,1,0:T(8,128)S(1)} all-to-all(f32[128,8,128]{2,1,0:T(8,128)S(1)} %shard_map.61), channel_id=1, replica_groups=mesh['dp'=8,'tensor'=16] {'dp','tensor'}, dimensions={0} | all-to-all | bytes 1048576 | tf_op jit(solution)/shard_map/all_to_all | solution.py:258
  56.3 0.1 shard_map.62
  56.4 18.1 %all_to_all.21.refs_0_ = f32[128,8,128]{2,1,0:T(8,128)S(1)} all-to-all(f32[128,8,128]{2,1,0:T(8,128)S(1)} %shard_map.62), channel_id=1, replica_groups=mesh['dp'=8,'tensor'=16] {'dp','tensor'}, dimensions={0} | all-to-all | bytes 1048576 | tf_op jit(solution)/shard_map/all_to_all | solution.py:260
  74.5 2.3 %shard_map.63 = (f32[32,4096]{1,0:T(8,128)S(1)}, bf16[96,4096]{1,0:T(8,128)(2,1)S(1)}, f32[16,32,128]{2,1,0:T(8,128)}) custom-call(f32[128,8,128]{2,1,0:T(8,128)S(1)} %all_to_all.21.refs_0_, bf16[4096,128]{1,0:T(8,128)(2,1)S(1)} %bitcast.11), custom_call_target="tpu_custom_call" | custom-call | flops 1048576 | bytes 65536 | tf_op jit(solution)/shard_map/pallas_call | solution.py:60
  76.8 3.5 %all-to-all-start.3 = ((f32[16,32,128]{2,1,0:T(8,128)}), f32[16,32,128]{2,1,0:T(8,128)S(1)}, u32[]{:S(2)}, u32[]{:S(2)}) async-start(f32[16,32,128]{2,1,0:T(8,128)} %get-tuple-element.14), calls=%async_computation.3 | async-start | bytes 524288 | tf_op jit(solution)/shard_map/all_to_all | solution.py:267
  80.3 0.0 copy-start.1
  80.3 3.2 %copy-done.1 = bf16[1,4096,896]{2,1,0:T(8,128)(2,1)S(1)} copy-done((bf16[1,4096,896]{2,1,0:T(8,128)(2,1)S(1)}, bf16[1,4096,896]{2,1,0:T(8,128)(2,1)}, u32[]{:S(2)}) %copy-start.1) | copy-done | bytes 7340056
  83.5 6.4 %shard_map.64 = (f32[32,896]{1,0:T(8,128)S(1)}, f32[32,32]{1,0:T(8,128)S(1)}, bf16[192,4096]{1,0:T(8,128)(2,1)S(1)}) custom-call(f32[32,4096]{1,0:T(8,128)S(1)} %get-tuple-element.10.refs_0_, bf16[96,4096]{1,0:T(8,128)(2,1)S(1)} %get-tuple-element.11.refs_1_, bf16[4096,896]{1,0:T(8,128)(2,1)S(1)} %bitcast.7), custom_call_target="tpu_custom_call" | custom-call | flops 1048576 | bytes 65536 | tf_op jit(solution)/shard_map/pallas_call | solution.py:60
  89.8 1.8 %all-to-all-done.3.refs_0_ = f32[16,32,128]{2,1,0:T(8,128)S(1)} async-done(((f32[16,32,128]{2,1,0:T(8,128)}), f32[16,32,128]{2,1,0:T(8,128)S(1)}, u32[]{:S(2)}, u32[]{:S(2)}) %all-to-all-start.3) | async-done | bytes 262176 | tf_op jit(solution)/shard_map/all_to_all | solution.py:267
  91.6 0.0 copy-start.4
  91.6 2.1 %copy-done.4 = bf16[2048,896]{1,0:T(8,128)(2,1)S(1)} copy-done((bf16[2048,896]{1,0:T(8,128)(2,1)S(1)}, bf16[2048,896]{1,0:T(8,128)(2,1)}, u32[]{:S(2)}) %copy-start.4) | copy-done | bytes 3670040
  93.7 1.2 shard_map.65
  95.0 1.7 collective-permute-start
  96.7 1.0 collective-permute-done
  97.7 0.5 collective-permute-start.3
  98.3 2.3 %collective-permute-start.2 = (f32[32,896]{1,0:T(8,128)S(1)}, f32[32,896]{1,0:T(8,128)S(1)}, u32[]{:S(2)}, u32[]{:S(2)}) collective-permute-start(f32[32,896]{1,0:T(8,128)S(1)} %add.3.refs_1_), channel_id=1, source_target_pairs={{64,0},{65,1},{66,2},{67,3},{68,4},{69,5},{70,6},{71,7},{72,8},{73... | collective-permute-start | bytes 344072 | tf_op jit(solution)/shard_map/ppermute | solution.py:32
  100.6 1.2 collective-permute-start.1
  101.8 1.7 collective-permute-done.3.refs_4_
  103.5 2.4 %collective-permute-done.2.refs_3_ = f32[32,896]{1,0:T(8,128)S(1)} collective-permute-done((f32[32,896]{1,0:T(8,128)S(1)}, f32[32,896]{1,0:T(8,128)S(1)}, u32[]{:S(2)}, u32[]{:S(2)}) %collective-permute-start.2) | collective-permute-done | bytes 114720 | tf_op jit(solution)/shard_map/ppermute | solution.py:32
  105.9 0.3 collective-permute-done.1.refs_2_
  106.2 0.9 shard_map.66
  107.1 33.6 %all-gather.3.cloned.1.call-done = bf16[65536,128]{1,0:T(8,128)(2,1)} async-done(((bf16[4096,128]{1,0:T(8,128)(2,1)}), bf16[65536,128]{1,0:T(8,128)(2,1)}) %all-gather.3.cloned.1.call-update) | async-done | bytes 16777232 | tf_op jit(solution)/shard_map/all_gather | solution.py:233
  140.7 0.0 copy-start.2
  140.7 3.1 %copy-done.2 = bf16[1,4096,896]{2,1,0:T(8,128)(2,1)S(1)} copy-done((bf16[1,4096,896]{2,1,0:T(8,128)(2,1)S(1)}, bf16[1,4096,896]{2,1,0:T(8,128)(2,1)}, u32[]{:S(2)}) %copy-start.2) | copy-done | bytes 7340056
  143.8 0.0 copy-start.5
  143.8 2.0 %copy-done.5 = bf16[2048,896]{1,0:T(8,128)(2,1)S(1)} copy-done((bf16[2048,896]{1,0:T(8,128)(2,1)S(1)}, bf16[2048,896]{1,0:T(8,128)(2,1)}, u32[]{:S(2)}) %copy-start.5) | copy-done | bytes 3670040
  145.8 23.8 %shard_map.67 = bf16[4096,896]{1,0:T(8,128)(2,1)} custom-call(bf16[16,4096,128]{2,1,0:T(8,128)(2,1)} %bitcast.14, bf16[2048,896]{1,0:T(8,128)(2,1)S(1)} %copy-done.5, bf16[192,4096]{1,0:T(8,128)(2,1)S(1)} %get-tuple-element.12.refs_2_, bf16[192,896]{1,0:T(8,128)(2,1)S(1)} %get-tuple-element.16.refs_3_, bf16[4096,896]{1,0:T(8,128)(2,1)S(1)} %bitcast.8), custom_call_target="tpu_custom_call" | custom-call | flops 1048576 | bytes 65536 | tf_op jit(solution)/shard_map/pallas_call | solution.py:60
  (1 shorter events, 0.0 us)
Async XLA Ops:
  7.2 16.5 %copy-start.8 = (f32[896,32]{0,1:T(8,128)S(1)}, f32[896,32]{0,1:T(8,128)}, u32[]{:S(2)}) copy-start(f32[896,32]{0,1:T(8,128)} %param.7) | copy-start | bytes 344068
  7.2 133.5 %all-gather.3.cloned.1.call-start = ((), (), s32[]{:S(2)}) async-start(), calls=%async_computation.4 | async-start | bytes 17825792 | tf_op jit(solution)/shard_map/all_gather | solution.py:233
  9.5 22.9 %copy-start.6 = (bf16[128,4096]{0,1:T(8,128)(2,1)S(1)}, bf16[128,4096]{0,1:T(8,128)(2,1)}, u32[]{:S(2)}) copy-start(bf16[128,4096]{0,1:T(8,128)(2,1)} %copy.6) | copy-start | bytes 3145732
  9.5 2.1 %copy-start.3 = (bf16[2048,896]{1,0:T(8,128)(2,1)S(1)}, bf16[2048,896]{1,0:T(8,128)(2,1)}, u32[]{:S(2)}) copy-start(bf16[2048,896]{1,0:T(8,128)(2,1)} %refs_1_.5) | copy-start | bytes 11010052
  11.6 0.9 copy-start.7
  15.0 17.4 %all-to-all-start = ((f32[16,32,128]{2,1,0:T(8,128)}), f32[16,32,128]{2,1,0:T(8,128)S(1)}, u32[]{:S(2)}, u32[]{:S(2)}) async-start(f32[16,32,128]{2,1,0:T(8,128)} %shard_map.59), calls=%async_computation | async-start | bytes 524288 | tf_op jit(solution)/shard_map/all_to_all | solution.py:241
  23.7 3.8 %copy-start = (bf16[1,4096,896]{2,1,0:T(8,128)(2,1)S(1)}, bf16[1,4096,896]{2,1,0:T(8,128)(2,1)}, u32[]{:S(2)}) copy-start(bf16[1,4096,896]{2,1,0:T(8,128)(2,1)} %param.6) | copy-start | bytes 22020100
  76.8 14.9 %all-to-all-start.3 = ((f32[16,32,128]{2,1,0:T(8,128)}), f32[16,32,128]{2,1,0:T(8,128)S(1)}, u32[]{:S(2)}, u32[]{:S(2)}) async-start(f32[16,32,128]{2,1,0:T(8,128)} %get-tuple-element.14), calls=%async_computation.3 | async-start | bytes 524288 | tf_op jit(solution)/shard_map/all_to_all | solution.py:267
  80.3 3.2 %copy-start.1 = (bf16[1,4096,896]{2,1,0:T(8,128)(2,1)S(1)}, bf16[1,4096,896]{2,1,0:T(8,128)(2,1)}, u32[]{:S(2)}) copy-start(bf16[1,4096,896]{2,1,0:T(8,128)(2,1)} %param.6) | copy-start | bytes 22020100
  91.6 2.1 %copy-start.4 = (bf16[2048,896]{1,0:T(8,128)(2,1)S(1)}, bf16[2048,896]{1,0:T(8,128)(2,1)}, u32[]{:S(2)}) copy-start(bf16[2048,896]{1,0:T(8,128)(2,1)} %refs_1_.5) | copy-start | bytes 11010052
  95.0 2.7 %collective-permute-start = (f32[32,896]{1,0:T(8,128)S(1)}, f32[32,896]{1,0:T(8,128)S(1)}, u32[]{:S(2)}, u32[]{:S(2)}) collective-permute-start(f32[32,896]{1,0:T(8,128)S(1)} %shard_map.65), channel_id=1, source_target_pairs={{16,0},{17,1},{18,2},{19,3},{20,4},{21,5},{22,6},{23,7},{24,8},{25... | collective-permute-start | bytes 344072 | tf_op jit(solution)/shard_map/ppermute | solution.py:32
  97.7 5.8 %collective-permute-start.3 = (f32[32,896]{1,0:T(8,128)S(1)}, f32[32,896]{1,0:T(8,128)S(1)}, u32[]{:S(2)}, u32[]{:S(2)}) collective-permute-start(f32[32,896]{1,0:T(8,128)S(1)} %add.3.refs_1_), channel_id=1, source_target_pairs={{96,0},{97,1},{98,2},{99,3},{100,4},{101,5},{102,6},{103,7},{104,8... | collective-permute-start | bytes 344072 | tf_op jit(solution)/shard_map/ppermute | solution.py:32
  98.3 7.7 %collective-permute-start.2 = (f32[32,896]{1,0:T(8,128)S(1)}, f32[32,896]{1,0:T(8,128)S(1)}, u32[]{:S(2)}, u32[]{:S(2)}) collective-permute-start(f32[32,896]{1,0:T(8,128)S(1)} %add.3.refs_1_), channel_id=1, source_target_pairs={{64,0},{65,1},{66,2},{67,3},{68,4},{69,5},{70,6},{71,7},{72,8},{73... | collective-permute-start | bytes 344072 | tf_op jit(solution)/shard_map/ppermute | solution.py:32
  100.6 5.6 %collective-permute-start.1 = (f32[32,896]{1,0:T(8,128)S(1)}, f32[32,896]{1,0:T(8,128)S(1)}, u32[]{:S(2)}, u32[]{:S(2)}) collective-permute-start(f32[32,896]{1,0:T(8,128)S(1)} %add.3.refs_1_), channel_id=1, source_target_pairs={{32,0},{33,1},{34,2},{35,3},{36,4},{37,5},{38,6},{39,7},{40,8},{41... | collective-permute-start | bytes 344072 | tf_op jit(solution)/shard_map/ppermute | solution.py:32
  140.7 3.1 %copy-start.2 = (bf16[1,4096,896]{2,1,0:T(8,128)(2,1)S(1)}, bf16[1,4096,896]{2,1,0:T(8,128)(2,1)}, u32[]{:S(2)}) copy-start(bf16[1,4096,896]{2,1,0:T(8,128)(2,1)} %param.6) | copy-start | bytes 22020100
  143.8 2.0 %copy-start.5 = (bf16[2048,896]{1,0:T(8,128)(2,1)S(1)}, bf16[2048,896]{1,0:T(8,128)(2,1)}, u32[]{:S(2)}) copy-start(bf16[2048,896]{1,0:T(8,128)(2,1)} %refs_1_.5) | copy-start | bytes 11010052
Sparse Core Ops, SparseCore 0:
  10.7 129.9 all-gather.2

commit v2 on v1

--- a/solution.py
+++ b/solution.py
@@ -10,7 +10,6 @@
 NX, NC, NZ, NY = 4, 2, 4, 4
 N_DP = NX * NC
 TOK = 128
-TILE = 128
 BLOCK = 512
 F32, BF16 = jnp.float32, jnp.bfloat16
 SMEM = pl.BlockSpec(memory_space=pltpu.SMEM)
@@ -49,7 +48,7 @@
     return pl.BlockSpec(tuple(array.shape), lambda *_: zeros)
 
 
-def kernel_call(body, grid, operands, in_specs, outs, out_specs, scratch=(), aliases=None, vmem_mib=24, after=()):
+def kernel_call(body, grid, operands, in_specs, outs, out_specs, scratch=(), aliases=None, vmem_mib=16, after=()):
     count = len(operands)
     operands = [*operands, *after]
     in_specs = [*in_specs, *[pl.BlockSpec(memory_space=pltpu.HBM)] * len(after)]
@@ -108,7 +107,7 @@
     out[...] = fold3(dot_nt(pieces[...], e[...]))
 
 
-def power_body(hq, ct, eq, out, lhs):
+def power_body(hq, c, eq, out, lhs):
     @pl.when(pl.program_id(0) == 0)
     def _():
         total = hq[0]
@@ -116,34 +115,42 @@
             total += hq[t]
         lhs[...] = split3(total)
 
-    term = fold3(dot_nt(lhs[...], ct[...])) + eq[...]
-    for j in range(BLOCK // TILE):
-        for i in range(RANK // 8):
-            out[j * (RANK // 8) + i] = term[i * 8:(i + 1) * 8, j * TILE:(j + 1) * TILE]
-
-
-def tile_sum_body(tiles, out):
-    totals = [tiles[k] for k in range(4)]
-    for k in range(4, tiles.shape[0]):
-        totals[k % 4] += tiles[k]
-    out[...] = jnp.broadcast_to(((totals[0] + totals[1]) + (totals[2] + totals[3]))[None], out.shape)
-
-
-def cp_body(tiles, ct, power, pieces, out, acc):
+    term = fold3(dot_nn(lhs[...], c[...])) + eq[...]
+    for j in range(out.shape[0]):
+        out[j] = term[:, j * BLOCK:(j + 1) * BLOCK]
+
+
+def sum_body(*refs):
+    total = refs[0][...]
+    for ref in refs[1:-1]:
+        total += ref[...]
+    refs[-1][...] = total
+
+
+def sum_copies_body(*refs):
+    total = (refs[0][...] + refs[1][...]) + (refs[2][...] + refs[3][...])
+    refs[4][...] = jnp.broadcast_to(total[None], refs[4].shape)
+
+
+def sum_pieces_body(pieces, out):
+    total = pieces[0]
+    for r in range(1, N_DP):
+        total += pieces[r]
+    out[...] = total
+
+
+def cp_body(power_pieces, c, power, pieces, out, acc):
     i = pl.program_id(0)
 
     @pl.when(i == 0)
     def _():
         acc[...] = jnp.zeros_like(acc)
 
-    n = RANK // 8
-    block = jnp.concatenate([
-        jnp.concatenate([tiles[j * n + k] for k in range(n)], axis=0) for j in range(BLOCK // TILE)
-    ], axis=1)
+    block = jnp.concatenate([power_pieces[j] for j in range(power_pieces.shape[0])], axis=1)
     power[...] = block
     split = split3(block)
     pieces[...] = split
-    acc[...] += fold3(dot_nn(split, ct[...]))
+    acc[...] += fold3(dot_nt(split, c[...]))
 
     @pl.when(i == pl.num_programs(0) - 1)
     def _():
@@ -205,21 +212,29 @@
     pieces[...] = jnp.concatenate([high, middle, high, low, high, middle], axis=0)
 
 
-def error_body(g, h, basis, q, e, out):
-    left = jnp.concatenate([g[t] for t in range(NZ * NY)], axis=1)
-    acc = dot_nn(left, h[...])
+def rest_body(basis, q, e, out):
     update = lax.dot_general(basis[...], q[...], (((0,), (0,)), ((), ())), preferred_element_type=F32)
-    out[...] = ((acc + e[...].astype(F32)) - update).astype(BF16)
-
-
-def error_call(gathered, h, basis, q, e):
+    out[...] = e[...].astype(F32) - update
+
+
+def error_body(c, h, rest, out):
+    gradient = lax.dot_general(c[...], h[...], (((0,), (0,)), ((), ())), preferred_element_type=F32)
+    out[...] = (gradient + rest[...]).astype(BF16)
+
+
+def error_calls(gathered, h, basis, q, e):
     rows, columns = e.shape
+    wide = 2 * BLOCK
+    in_rows = pl.BlockSpec((wide, columns), lambda i: (i, 0))
+    (rest,) = kernel_call(
+        rest_body, rows // wide, [basis, q, e],
+        [pl.BlockSpec((basis.shape[0], wide), lambda i: (0, i)), None, in_rows], [f32(rows, columns)], [in_rows], vmem_mib=56,
+    )
     in_rows = pl.BlockSpec((BLOCK, columns), lambda i: (i, 0))
     return kernel_call(
-        error_body, rows // BLOCK, [gathered, h, basis, q, e],
-        [pl.BlockSpec((NZ * NY, BLOCK, TOK), lambda i: (0, i, 0)), None,
-         pl.BlockSpec((basis.shape[0], BLOCK), lambda i: (0, i)), None, in_rows],
-        [bf16(rows, columns)], [in_rows], vmem_mib=40,
+        error_body, rows // BLOCK, [gathered, h, rest],
+        [pl.BlockSpec((gathered.shape[0], BLOCK), lambda i: (0, i)), None, in_rows],
+        [bf16(rows, columns)], [in_rows], vmem_mib=56,
     )[0]
 
 
@@ -229,8 +244,7 @@
     columns = hidden.shape[1]
     n_blocks = rows // BLOCK
 
-    ct = cotangent.T
-    gathered = lax.all_gather(ct, "tensor", axis=0)
+    gathered = lax.all_gather(cotangent, "tensor", axis=0, tiled=True)
 
     q_t = q_start.T
     (hq,) = kernel_call(
@@ -248,20 +262,25 @@
     stack_specs = [
         pl.BlockSpec((BLOCK, 4 * TOK), lambda i, n=n: (jnp.clip(i - 2 * n, 0, 1), 0)) for n in range(4)
     ]
-    ct_spec = pl.BlockSpec((BLOCK, TOK), lambda i: (i, 0))
-    n_tiles = RANK // 8 * (rows // TILE)
-    tile_spec = pl.BlockSpec((n_tiles // n_blocks, 8, TILE), lambda i: (i, 0, 0))
-    (tiles,) = kernel_call(
-        power_body, n_blocks, [hq, ct, eq], [None, ct_spec, column_spec], [f32(n_tiles, 8, TILE)], [tile_spec],
+    wide = n_blocks // 2
+    c_spec = pl.BlockSpec((TOK, wide * BLOCK), lambda i: (0, i))
+    wide_spec = pl.BlockSpec((RANK, wide * BLOCK), lambda i: (0, i))
+    piece_spec = pl.BlockSpec((wide, RANK, BLOCK), lambda i: (i, 0, 0))
+    (terms,) = kernel_call(
+        power_body, 2, [hq, cotangent, eq], [None, c_spec, wide_spec], [f32(N_DP, RANK, BLOCK)], [piece_spec],
         scratch=[pltpu.VMEM((3 * RANK, TOK), BF16)],
     )
-    tiles = lax.all_to_all(tiles, AXES, 0, 0)
-    (tiles,) = kernel_call(tile_sum_body, 1, [tiles], [None], [f32(n_tiles, 8, TILE)], [None])
-    tiles = lax.all_to_all(tiles, AXES, 0, 0)
+    terms = lax.all_to_all(terms, "dp", 0, 0)
+    (piece,) = kernel_call(sum_pieces_body, 1, [terms], [None], [f32(RANK, BLOCK)], [None])
+    (piece,) = kernel_call(sum_body, 1, around([piece] * 4, "y"), [None] * 4, [f32(RANK, BLOCK)], [None])
+    (copies,) = kernel_call(
+        sum_copies_body, 1, around([piece] * 4, "z"), [None] * 4, [f32(N_DP, RANK, BLOCK)], [None],
+    )
+    power_pieces = lax.all_to_all(copies, "dp", 0, 0)
     power, pieces, cp = kernel_call(
-        cp_body, n_blocks, [tiles, ct], [tile_spec, ct_spec],
+        cp_body, 2, [power_pieces, cotangent], [piece_spec, c_spec],
         [f32(RANK, rows), bf16(3 * RANK, rows), f32(NZ * NY, RANK, TOK)],
-        [column_spec, pl.BlockSpec((3 * RANK, BLOCK), lambda i: (0, i)), None],
+        [wide_spec, pl.BlockSpec((3 * RANK, wide * BLOCK), lambda i: (0, i)), None],
         scratch=[pltpu.VMEM((RANK, TOK), F32)],
     )
     cp = lax.all_to_all(cp, "tensor", 0, 0)
@@ -282,7 +301,7 @@
         [f32(RANK, columns), bf16(6 * RANK, columns)], [None] * 2,
     )
 
-    out = error_call(gathered, hidden, basis, q_pieces, error)
+    out = error_calls(gathered, hidden, basis, q_pieces, error)
     return out[None], q_mean.T
 
 

time: 177 us -> 162 us (0.915)
  waiting for transfers between devices: 42.3 us -> 21.4 us
  starting transfers between devices: 18 us -> 28.8 us
  blocking collectives: 40.4 us -> 31.4 us
  Pallas kernels: 42.2 us -> 50.4 us
  local copies, waits for them, and re-layouts: 19.5 us -> 14.8 us
    all_gather x1, waiting for transfers between devices: 33.6 us -> 6.88 us  [on_device(): gathered = lax.all_gather(cotangent, 'tensor', axis=0, tiled=True)]
    all_to_all x2, blocking collectives: 40.4 us -> 31.4 us  [the longest x1 16.4 us: on_device(): terms = lax.all_to_all(terms, 'dp', 0, 0)]
    pallas_call x9 -> x12, Pallas kernels: 42.2 us -> 50.4 us  [kernel_call(): pl.pallas_call(call, grid=(grid,), in_specs=[whole(a) if s is None else s...]
    ppermute x4 -> x10, starting transfers between devices: 5.79 us -> 14 us  [fetch(): return lax.ppermute(array, AXES, receive_from(**offsets))]
    ppermute x4 -> x10, waiting for transfers between devices: 5.39 us -> 13.3 us  [fetch(): return lax.ppermute(array, AXES, receive_from(**offsets))]
    unnamed x19 -> x18, local copies, waits for them, and re-layouts: 19.5 us -> 14.8 us
    all_to_all x1, starting transfers between devices: 3.53 us -> 6.16 us  [on_device(): cp = lax.all_to_all(cp, 'tensor', 0, 0)]
  transfers between devices with their start and end apart: 7 -> 13, of which waited for: 7 -> 10; matrix products, arithmetic and copies ran while one was open for 0% -> 0% of each run, Pallas kernels for 10% -> 17%
where the time goes in v2:
time: 162 us; the launch traced here: 161 us
  Pallas kernels  50.4 us (31%)
  blocking collectives  31.4 us (19%)
  starting transfers between devices  28.8 us (18%)
  waiting for transfers between devices  21.4 us (13%)
  local copies, waits for them, and re-layouts  14.8 us (9%)
  between operations  14.2 us (9%)
    pallas_call x12, Pallas kernels, kernel_call(): pl.pallas_call(call, grid=(grid,), in_specs=[whole(a) if s is None else s...  50.4 us
    all_to_all x1, blocking collectives, on_device(): terms = lax.all_to_all(terms, 'dp', 0, 0)  16.4 us
    all_to_all x1, blocking collectives, on_device(): power_pieces = lax.all_to_all(copies, 'dp', 0, 0)  15 us
    unnamed x18, local copies, waits for them, and re-layouts  14.8 us
    ppermute x10, starting transfers between devices, fetch(): return lax.ppermute(array, AXES, receive_from(**offsets))  14 us
    ppermute x10, waiting for transfers between devices, fetch(): return lax.ppermute(array, AXES, receive_from(**offsets))  13.3 us
    all_to_all x1, starting transfers between devices, on_device(): hq = lax.all_to_all(hq, 'tensor', 0, 0)  8.59 us
    all_gather x1, waiting for transfers between devices, on_device(): gathered = lax.all_gather(cotangent, 'tensor', axis=0, tiled=True)  6.88 us
  transfers between devices with their start and end apart: 13, of which 10 were waited for; matrix products, arithmetic and copies ran while one was open for 0% of the time, Pallas kernels for 17%

profile of v2, /device:TPU:1, one launch (start us, length us, event | category | flops | bytes accessed | tf_op | source)
XLA Modules:
  0.0 161.0 jit_solution(10968940003080040331)
XLA Ops:
  7.2 0.0 copy-start.4
  7.2 0.0 all-gather.2.cloned.1.call-start
  7.2 0.7 all-gather.2.cloned.1.call-update
  7.9 0.0 copy-start.2
  7.9 2.0 %copy-done.2 = bf16[2048,896]{1,0:T(8,128)(2,1)S(1)} copy-done((bf16[2048,896]{1,0:T(8,128)(2,1)S(1)}, bf16[2048,896]{1,0:T(8,128)(2,1)}, u32[]{:S(2)}) %copy-start.2) | copy-done | bytes 3670040
  9.9 0.0 copy-start.6
  10.0 0.9 copy-done.6
  10.8 2.5 %shard_map.59 = f32[16,32,128]{2,1,0:T(8,128)} custom-call(f32[32,896]{1,0:T(8,128)S(1)} %bitcast.7, bf16[2048,896]{1,0:T(8,128)(2,1)S(1)} %copy-done.2), custom_call_target="tpu_custom_call" | custom-call | flops 1048576 | bytes 65536 | tf_op jit(solution)/shard_map/pallas_call | solution.py:59
  13.4 8.6 %all-to-all-start = ((f32[16,32,128]{2,1,0:T(8,128)}), f32[16,32,128]{2,1,0:T(8,128)S(1)}, u32[]{:S(2)}, u32[]{:S(2)}) async-start(f32[16,32,128]{2,1,0:T(8,128)} %shard_map.59), calls=%async_computation | async-start | bytes 524288 | tf_op jit(solution)/shard_map/all_to_all | solution.py:255
  22.0 0.0 copy-start
  22.0 3.8 %copy-done = bf16[1,4096,896]{2,1,0:T(8,128)(2,1)S(1)} copy-done((bf16[1,4096,896]{2,1,0:T(8,128)(2,1)S(1)}, bf16[1,4096,896]{2,1,0:T(8,128)(2,1)}, u32[]{:S(2)}) %copy-start) | copy-done | bytes 7340056
  25.8 0.0 copy-start.7
  25.8 0.9 copy-done.7
  26.7 3.4 %shard_map.60.refs_2_ = f32[32,4096]{1,0:T(8,128)S(1)} custom-call(f32[32,896]{1,0:T(8,128)S(1)} %bitcast.8, bf16[4096,896]{1,0:T(8,128)(2,1)S(1)} %bitcast.5), custom_call_target="tpu_custom_call" | custom-call | flops 1048576 | bytes 65536 | tf_op jit(solution)/shard_map/pallas_call | solution.py:59
  30.1 0.0 all-to-all-done.refs_0_
  30.1 0.0 copy-done.4
  30.1 0.7 shard_map.61
  30.8 16.4 %all_to_all.20.refs_0_ = f32[8,32,512]{2,1,0:T(8,128)S(1)} all-to-all(f32[8,32,512]{2,1,0:T(8,128)S(1)} %shard_map.61), channel_id=1, replica_groups=mesh['dp'=8,'tensor'=16] {'dp'}, dimensions={0} | all-to-all | bytes 1048576 | tf_op jit(solution)/shard_map/all_to_all | solution.py:273
  47.2 0.1 collective-permute-start.2
  47.3 2.1 %collective-permute-start.1 = (f32[32,512]{1,0:T(8,128)S(1)}, f32[32,512]{1,0:T(8,128)S(1)}, u32[]{:S(2)}, u32[]{:S(2)}) collective-permute-start(f32[32,512]{1,0:T(8,128)S(1)} %shard_map.62.refs_0_), channel_id=1, source_target_pairs={{2,0},{3,1},{0,2},{1,3},{6,4},{7,5},{4,6},{5,7},{10,8},{11,9},{8,1... | collective-permute-start | bytes 196616 | tf_op jit(solution)/shard_map/ppermute | solution.py:31
  49.5 1.2 collective-permute-start
  50.6 1.7 %collective-permute-done.2.refs_3_ = f32[32,512]{1,0:T(8,128)S(1)} collective-permute-done((f32[32,512]{1,0:T(8,128)S(1)}, f32[32,512]{1,0:T(8,128)S(1)}, u32[]{:S(2)}, u32[]{:S(2)}) %collective-permute-start.2) | collective-permute-done | bytes 65568 | tf_op jit(solution)/shard_map/ppermute | solution.py:31
  52.3 0.0 collective-permute-done.1.refs_2_
  52.3 0.9 collective-permute-done.refs_1_
  53.2 1.6 collective-permute-start.5
  54.8 2.4 %collective-permute-start.4 = (f32[32,512]{1,0:T(8,128)S(1)}, f32[32,512]{1,0:T(8,128)S(1)}, u32[]{:S(2)}, u32[]{:S(2)}) collective-permute-start(f32[32,512]{1,0:T(8,128)S(1)} %shard_map.63.refs_0_), channel_id=1, source_target_pairs={{8,0},{9,1},{10,2},{11,3},{12,4},{13,5},{14,6},{15,7},{0,8},{1,9},... | collective-permute-start | bytes 196616 | tf_op jit(solution)/shard_map/ppermute | solution.py:31
  57.2 1.2 collective-permute-start.3
  58.4 0.4 collective-permute-done.5.refs_3_
  58.7 3.8 %collective-permute-done.4.refs_2_ = f32[32,512]{1,0:T(8,128)S(1)} collective-permute-done((f32[32,512]{1,0:T(8,128)S(1)}, f32[32,512]{1,0:T(8,128)S(1)}, u32[]{:S(2)}, u32[]{:S(2)}) %collective-permute-start.4) | collective-permute-done | bytes 65568 | tf_op jit(solution)/shard_map/ppermute | solution.py:31
  62.6 0.0 collective-permute-done.3.refs_1_
  62.6 15.0 %all_to_all.21.refs_0_ = f32[8,32,512]{2,1,0:T(8,128)S(1)} all-to-all(f32[8,32,512]{2,1,0:T(8,128)S(1)} %shard_map.64), channel_id=1, replica_groups=mesh['dp'=8,'tensor'=16] {'dp'}, dimensions={0} | all-to-all | bytes 1048576 | tf_op jit(solution)/shard_map/all_to_all | solution.py:279
  77.6 1.6 shard_map.65
  79.2 6.2 %all-to-all-start.3 = ((f32[16,32,128]{2,1,0:T(8,128)}), f32[16,32,128]{2,1,0:T(8,128)S(1)}, u32[]{:S(2)}, u32[]{:S(2)}) async-start(f32[16,32,128]{2,1,0:T(8,128)} %get-tuple-element.14), calls=%async_computation.3 | async-start | bytes 524288 | tf_op jit(solution)/shard_map/all_to_all | solution.py:286
  85.3 0.0 copy-start.1
  85.3 3.1 %copy-done.1 = bf16[1,4096,896]{2,1,0:T(8,128)(2,1)S(1)} copy-done((bf16[1,4096,896]{2,1,0:T(8,128)(2,1)S(1)}, bf16[1,4096,896]{2,1,0:T(8,128)(2,1)}, u32[]{:S(2)}) %copy-start.1) | copy-done | bytes 7340056
  88.5 6.4 %shard_map.66 = (f32[32,896]{1,0:T(8,128)S(1)}, f32[32,32]{1,0:T(8,128)S(1)}, bf16[192,4096]{1,0:T(8,128)(2,1)S(1)}) custom-call(f32[32,4096]{1,0:T(8,128)S(1)} %get-tuple-element.10.refs_0_, bf16[96,4096]{1,0:T(8,128)(2,1)S(1)} %get-tuple-element.11.refs_1_, bf16[4096,896]{1,0:T(8,128)(2,1)S(1)} %bitcast.6), custom_call_target="tpu_custom_call" | custom-call | flops 1048576 | bytes 65536 | tf_op jit(solution)/shard_map/pallas_call | solution.py:59
  94.8 0.0 copy-start.5
  94.8 1.1 copy-done.5
  96.0 0.5 all-to-all-done.3.refs_0_
  96.5 0.0 copy-start.3
  96.5 2.2 %copy-done.3 = bf16[2048,896]{1,0:T(8,128)(2,1)S(1)} copy-done((bf16[2048,896]{1,0:T(8,128)(2,1)S(1)}, bf16[2048,896]{1,0:T(8,128)(2,1)}, u32[]{:S(2)}) %copy-start.3) | copy-done | bytes 3670040
  98.7 1.2 shard_map.67
  99.9 2.5 %collective-permute-start.6 = (f32[32,896]{1,0:T(8,128)S(1)}, f32[32,896]{1,0:T(8,128)S(1)}, u32[]{:S(2)}, u32[]{:S(2)}) collective-permute-start(f32[32,896]{1,0:T(8,128)S(1)} %shard_map.67), channel_id=1, source_target_pairs={{16,0},{17,1},{18,2},{19,3},{20,4},{21,5},{22,6},{23,7},{24,8},{25... | collective-permute-start | bytes 344072 | tf_op jit(solution)/shard_map/ppermute | solution.py:31
  102.4 1.0 collective-permute-done.6
  103.4 0.5 collective-permute-start.9
  103.9 1.7 %collective-permute-start.8 = (f32[32,896]{1,0:T(8,128)S(1)}, f32[32,896]{1,0:T(8,128)S(1)}, u32[]{:S(2)}, u32[]{:S(2)}) collective-permute-start(f32[32,896]{1,0:T(8,128)S(1)} %add.3.refs_1_), channel_id=1, source_target_pairs={{64,0},{65,1},{66,2},{67,3},{68,4},{69,5},{70,6},{71,7},{72,8},{73... | collective-permute-start | bytes 344072 | tf_op jit(solution)/shard_map/ppermute | solution.py:31
  105.5 0.8 collective-permute-start.7
  106.4 3.3 %collective-permute-done.9.refs_4_ = f32[32,896]{1,0:T(8,128)S(1)} collective-permute-done((f32[32,896]{1,0:T(8,128)S(1)}, f32[32,896]{1,0:T(8,128)S(1)}, u32[]{:S(2)}, u32[]{:S(2)}) %collective-permute-start.9) | collective-permute-done | bytes 114720 | tf_op jit(solution)/shard_map/ppermute | solution.py:31
  109.7 1.2 collective-permute-done.8.refs_3_
  110.9 1.0 collective-permute-done.7.refs_2_
  111.9 0.9 shard_map.68
  112.9 0.0 copy-start.8
  112.9 0.7 copy-done.8
  113.6 10.1 %shard_map.69.refs_2_ = f32[4096,896]{1,0:T(8,128)} custom-call(bf16[192,4096]{1,0:T(8,128)(2,1)} %copy-done.5, bf16[192,896]{1,0:T(8,128)(2,1)} %copy-done.8, bf16[4096,896]{1,0:T(8,128)(2,1)} %bitcast.4), custom_call_target="tpu_custom_call" | custom-call | flops 1048576 | bytes 65536 | tf_op jit(solution)/shard_map/pallas_call | solution.py:59
  123.7 6.9 %all-gather.2.cloned.1.call-done.refs_0_ = bf16[2048,4096]{1,0:T(8,128)(2,1)} async-done(((bf16[128,4096]{1,0:T(8,128)(2,1)}), bf16[2048,4096]{1,0:T(8,128)(2,1)}) %all-gather.2.cloned.1.call-update) | async-done | bytes 16777232 | tf_op jit(solution)/shard_map/all_gather | solution.py:247
  130.6 23.5 %shard_map.70 = bf16[4096,896]{1,0:T(8,128)(2,1)} custom-call(bf16[2048,4096]{1,0:T(8,128)(2,1)} %all-gather.2.cloned.1.call-done.refs_0_, bf16[2048,896]{1,0:T(8,128)(2,1)} %refs_1_.9, f32[4096,896]{1,0:T(8,128)} %shard_map.69.refs_2_), custom_call_target="tpu_custom_call" | custom-call | flops 1048576 | bytes 65536 | tf_op jit(solution)/shard_map/pallas_call | solution.py:59
  (4 shorter events, 0.1 us)
Async XLA Ops:
  7.2 22.9 %copy-start.4 = (bf16[128,4096]{1,0:T(8,128)(2,1)S(1)}, bf16[128,4096]{1,0:T(8,128)(2,1)}, u32[]{:S(2)}) copy-start(bf16[128,4096]{1,0:T(8,128)(2,1)} %refs_1_.7) | copy-start | bytes 3145732
  7.2 123.4 %all-gather.2.cloned.1.call-start = ((), (), s32[]{:S(2)}) async-start(), calls=%async_computation.4 | async-start | bytes 17825792 | tf_op jit(solution)/shard_map/all_gather | solution.py:247
  7.9 2.0 %copy-start.2 = (bf16[2048,896]{1,0:T(8,128)(2,1)S(1)}, bf16[2048,896]{1,0:T(8,128)(2,1)}, u32[]{:S(2)}) copy-start(bf16[2048,896]{1,0:T(8,128)(2,1)} %refs_1_.9) | copy-start | bytes 11010052
  9.9 0.9 copy-start.6
  13.4 16.7 %all-to-all-start = ((f32[16,32,128]{2,1,0:T(8,128)}), f32[16,32,128]{2,1,0:T(8,128)S(1)}, u32[]{:S(2)}, u32[]{:S(2)}) async-start(f32[16,32,128]{2,1,0:T(8,128)} %shard_map.59), calls=%async_computation | async-start | bytes 524288 | tf_op jit(solution)/shard_map/all_to_all | solution.py:255
  22.0 3.8 %copy-start = (bf16[1,4096,896]{2,1,0:T(8,128)(2,1)S(1)}, bf16[1,4096,896]{2,1,0:T(8,128)(2,1)}, u32[]{:S(2)}) copy-start(bf16[1,4096,896]{2,1,0:T(8,128)(2,1)} %param.6) | copy-start | bytes 22020100
  25.8 0.9 copy-start.7
  47.2 5.1 %collective-permute-start.2 = (f32[32,512]{1,0:T(8,128)S(1)}, f32[32,512]{1,0:T(8,128)S(1)}, u32[]{:S(2)}, u32[]{:S(2)}) collective-permute-start(f32[32,512]{1,0:T(8,128)S(1)} %shard_map.62.refs_0_), channel_id=1, source_target_pairs={{3,0},{0,1},{1,2},{2,3},{7,4},{4,5},{5,6},{6,7},{11,8},{8,9},{9,10... | collective-permute-start | bytes 196616 | tf_op jit(solution)/shard_map/ppermute | solution.py:31
  47.3 5.0 %collective-permute-start.1 = (f32[32,512]{1,0:T(8,128)S(1)}, f32[32,512]{1,0:T(8,128)S(1)}, u32[]{:S(2)}, u32[]{:S(2)}) collective-permute-start(f32[32,512]{1,0:T(8,128)S(1)} %shard_map.62.refs_0_), channel_id=1, source_target_pairs={{2,0},{3,1},{0,2},{1,3},{6,4},{7,5},{4,6},{5,7},{10,8},{11,9},{8,1... | collective-permute-start | bytes 196616 | tf_op jit(solution)/shard_map/ppermute | solution.py:31
  49.5 3.8 %collective-permute-start = (f32[32,512]{1,0:T(8,128)S(1)}, f32[32,512]{1,0:T(8,128)S(1)}, u32[]{:S(2)}, u32[]{:S(2)}) collective-permute-start(f32[32,512]{1,0:T(8,128)S(1)} %shard_map.62.refs_0_), channel_id=1, source_target_pairs={{1,0},{2,1},{3,2},{0,3},{5,4},{6,5},{7,6},{4,7},{9,8},{10,9},{11,1... | collective-permute-start | bytes 196616 | tf_op jit(solution)/shard_map/ppermute | solution.py:31
  53.2 5.5 %collective-permute-start.5 = (f32[32,512]{1,0:T(8,128)S(1)}, f32[32,512]{1,0:T(8,128)S(1)}, u32[]{:S(2)}, u32[]{:S(2)}) collective-permute-start(f32[32,512]{1,0:T(8,128)S(1)} %shard_map.63.refs_0_), channel_id=1, source_target_pairs={{12,0},{13,1},{14,2},{15,3},{0,4},{1,5},{2,6},{3,7},{4,8},{5,9},{6... | collective-permute-start | bytes 196616 | tf_op jit(solution)/shard_map/ppermute | solution.py:31
  54.8 7.8 %collective-permute-start.4 = (f32[32,512]{1,0:T(8,128)S(1)}, f32[32,512]{1,0:T(8,128)S(1)}, u32[]{:S(2)}, u32[]{:S(2)}) collective-permute-start(f32[32,512]{1,0:T(8,128)S(1)} %shard_map.63.refs_0_), channel_id=1, source_target_pairs={{8,0},{9,1},{10,2},{11,3},{12,4},{13,5},{14,6},{15,7},{0,8},{1,9},... | collective-permute-start | bytes 196616 | tf_op jit(solution)/shard_map/ppermute | solution.py:31
  57.2 5.4 %collective-permute-start.3 = (f32[32,512]{1,0:T(8,128)S(1)}, f32[32,512]{1,0:T(8,128)S(1)}, u32[]{:S(2)}, u32[]{:S(2)}) collective-permute-start(f32[32,512]{1,0:T(8,128)S(1)} %shard_map.63.refs_0_), channel_id=1, source_target_pairs={{4,0},{5,1},{6,2},{7,3},{8,4},{9,5},{10,6},{11,7},{12,8},{13,9},{1... | collective-permute-start | bytes 196616 | tf_op jit(solution)/shard_map/ppermute | solution.py:31
  79.2 17.3 %all-to-all-start.3 = ((f32[16,32,128]{2,1,0:T(8,128)}), f32[16,32,128]{2,1,0:T(8,128)S(1)}, u32[]{:S(2)}, u32[]{:S(2)}) async-start(f32[16,32,128]{2,1,0:T(8,128)} %get-tuple-element.14), calls=%async_computation.3 | async-start | bytes 524288 | tf_op jit(solution)/shard_map/all_to_all | solution.py:286
  85.3 3.1 %copy-start.1 = (bf16[1,4096,896]{2,1,0:T(8,128)(2,1)S(1)}, bf16[1,4096,896]{2,1,0:T(8,128)(2,1)}, u32[]{:S(2)}) copy-start(bf16[1,4096,896]{2,1,0:T(8,128)(2,1)} %param.6) | copy-start | bytes 22020100
  94.8 1.1 copy-start.5
  96.5 2.2 %copy-start.3 = (bf16[2048,896]{1,0:T(8,128)(2,1)S(1)}, bf16[2048,896]{1,0:T(8,128)(2,1)}, u32[]{:S(2)}) copy-start(bf16[2048,896]{1,0:T(8,128)(2,1)} %refs_1_.9) | copy-start | bytes 11010052
  99.9 3.4 %collective-permute-start.6 = (f32[32,896]{1,0:T(8,128)S(1)}, f32[32,896]{1,0:T(8,128)S(1)}, u32[]{:S(2)}, u32[]{:S(2)}) collective-permute-start(f32[32,896]{1,0:T(8,128)S(1)} %shard_map.67), channel_id=1, source_target_pairs={{16,0},{17,1},{18,2},{19,3},{20,4},{21,5},{22,6},{23,7},{24,8},{25... | collective-permute-start | bytes 344072 | tf_op jit(solution)/shard_map/ppermute | solution.py:31
  103.4 6.3 %collective-permute-start.9 = (f32[32,896]{1,0:T(8,128)S(1)}, f32[32,896]{1,0:T(8,128)S(1)}, u32[]{:S(2)}, u32[]{:S(2)}) collective-permute-start(f32[32,896]{1,0:T(8,128)S(1)} %add.3.refs_1_), channel_id=1, source_target_pairs={{96,0},{97,1},{98,2},{99,3},{100,4},{101,5},{102,6},{103,7},{104,8... | collective-permute-start | bytes 344072 | tf_op jit(solution)/shard_map/ppermute | solution.py:31
  103.9 7.0 %collective-permute-start.8 = (f32[32,896]{1,0:T(8,128)S(1)}, f32[32,896]{1,0:T(8,128)S(1)}, u32[]{:S(2)}, u32[]{:S(2)}) collective-permute-start(f32[32,896]{1,0:T(8,128)S(1)} %add.3.refs_1_), channel_id=1, source_target_pairs={{64,0},{65,1},{66,2},{67,3},{68,4},{69,5},{70,6},{71,7},{72,8},{73... | collective-permute-start | bytes 344072 | tf_op jit(solution)/shard_map/ppermute | solution.py:31
  105.5 6.4 %collective-permute-start.7 = (f32[32,896]{1,0:T(8,128)S(1)}, f32[32,896]{1,0:T(8,128)S(1)}, u32[]{:S(2)}, u32[]{:S(2)}) collective-permute-start(f32[32,896]{1,0:T(8,128)S(1)} %add.3.refs_1_), channel_id=1, source_target_pairs={{32,0},{33,1},{34,2},{35,3},{36,4},{37,5},{38,6},{39,7},{40,8},{41... | collective-permute-start | bytes 344072 | tf_op jit(solution)/shard_map/ppermute | solution.py:31
  112.9 0.8 copy-start.8
Sparse Core Ops, SparseCore 0:
  10.1 120.4 all-gather.1

commit v3 on v2

--- a/solution.py
+++ b/solution.py
@@ -217,12 +217,16 @@
     out[...] = e[...].astype(F32) - update
 
 
-def error_body(c, h, rest, out):
-    gradient = lax.dot_general(c[...], h[...], (((0,), (0,)), ((), ())), preferred_element_type=F32)
-    out[...] = (gradient + rest[...]).astype(BF16)
-
-
-def error_calls(gathered, h, basis, q, e):
+def turn_body(h, out):
+    out[...] = h[...].T
+
+
+def error_body(c, h_t, rest, out):
+    gradient = dot_nn(h_t[...], c[...])
+    out[...] = (gradient.T + rest[...]).astype(BF16)
+
+
+def error_calls(gathered, h_t, basis, q, e):
     rows, columns = e.shape
     wide = 2 * BLOCK
     in_rows = pl.BlockSpec((wide, columns), lambda i: (i, 0))
@@ -230,10 +234,9 @@
         rest_body, rows // wide, [basis, q, e],
         [pl.BlockSpec((basis.shape[0], wide), lambda i: (0, i)), None, in_rows], [f32(rows, columns)], [in_rows], vmem_mib=56,
     )
-    in_rows = pl.BlockSpec((BLOCK, columns), lambda i: (i, 0))
     return kernel_call(
-        error_body, rows // BLOCK, [gathered, h, rest],
-        [pl.BlockSpec((gathered.shape[0], BLOCK), lambda i: (0, i)), None, in_rows],
+        error_body, rows // wide, [gathered, h_t, rest],
+        [pl.BlockSpec((gathered.shape[0], wide), lambda i: (0, i)), None, in_rows],
         [bf16(rows, columns)], [in_rows], vmem_mib=56,
     )[0]
 
@@ -271,7 +274,11 @@
         scratch=[pltpu.VMEM((3 * RANK, TOK), BF16)],
     )
     terms = lax.all_to_all(terms, "dp", 0, 0)
-    (piece,) = kernel_call(sum_pieces_body, 1, [terms], [None], [f32(RANK, BLOCK)], [None])
+    (hidden_t,) = kernel_call(
+        turn_body, NZ, [hidden], [pl.BlockSpec((4 * TOK, columns), lambda i: (i, 0))], [bf16(columns, hidden.shape[0])],
+        [pl.BlockSpec((columns, 4 * TOK), lambda i: (0, i))], vmem_mib=56, after=[eq],
+    )
+    (piece,) = kernel_call(sum_pieces_body, 1, [terms], [None], [f32(RANK, BLOCK)], [None], after=[hidden_t])
     (piece,) = kernel_call(sum_body, 1, around([piece] * 4, "y"), [None] * 4, [f32(RANK, BLOCK)], [None])
     (copies,) = kernel_call(
         sum_copies_body, 1, around([piece] * 4, "z"), [None] * 4, [f32(N_DP, RANK, BLOCK)], [None],
@@ -301,7 +308,7 @@
         [f32(RANK, columns), bf16(6 * RANK, columns)], [None] * 2,
     )
 
-    out = error_calls(gathered, hidden, basis, q_pieces, error)
+    out = error_calls(gathered, hidden_t, basis, q_pieces, error)
     return out[None], q_mean.T
 
 

time: 162 us -> 161 us (level)
  blocking collectives: 31.4 us -> 16.7 us
  starting transfers between devices: 28.8 us -> 34.7 us
  Pallas kernels: 50.4 us -> 55.3 us
  local copies, waits for them, and re-layouts: 14.8 us -> 16.9 us
    all_to_all x1 -> x0, blocking collectives: 16.4 us -> none  [on_device(): terms = lax.all_to_all(terms, 'dp', 0, 0)]
    all_to_all x0 -> x1, starting transfers between devices: none -> 7.22 us  [on_device(): terms = lax.all_to_all(terms, 'dp', 0, 0)]
    pallas_call x12 -> x13, Pallas kernels: 50.4 us -> 55.3 us  [kernel_call(): pl.pallas_call(call, grid=(grid,), in_specs=[whole(a) if s is None else s...]
    all_to_all x0 -> x1, waiting for transfers between devices: none -> 4.43 us  [on_device(): terms = lax.all_to_all(terms, 'dp', 0, 0)]
    all_gather x1, waiting for transfers between devices: 6.88 us -> 2.83 us  [on_device(): gathered = lax.all_gather(cotangent, 'tensor', axis=0, tiled=True)]
    unnamed x18 -> x22, local copies, waits for them, and re-layouts: 14.8 us -> 16.9 us
    all_to_all x1, blocking collectives: 15 us -> 16.7 us  [on_device(): power_pieces = lax.all_to_all(copies, 'dp', 0, 0)]
  transfers between devices with their start and end apart: 13 -> 14, of which waited for: 10 -> 13; matrix products, arithmetic and copies ran while one was open for 0% -> 0% of each run, Pallas kernels for 17% -> 20%
where the time goes in v3:
time: 161 us; the launch traced here: 160 us
  Pallas kernels  55.3 us (34%)
  starting transfers between devices  34.7 us (22%)
  waiting for transfers between devices  22.6 us (14%)
  local copies, waits for them, and re-layouts  16.9 us (10%)
  blocking collectives  16.7 us (10%)
  between operations  14.2 us (9%)
    pallas_call x13, Pallas kernels, kernel_call(): pl.pallas_call(call, grid=(grid,), in_specs=[whole(a) if s is None else s...  55.3 us
    unnamed x22, local copies, waits for them, and re-layouts  16.9 us
    all_to_all x1, blocking collectives, on_device(): power_pieces = lax.all_to_all(copies, 'dp', 0, 0)  16.7 us
    ppermute x10, waiting for transfers between devices, fetch(): return lax.ppermute(array, AXES, receive_from(**offsets))  14.4 us
    ppermute x10, starting transfers between devices, fetch(): return lax.ppermute(array, AXES, receive_from(**offsets))  13.3 us
    all_to_all x1, starting transfers between devices, on_device(): hq = lax.all_to_all(hq, 'tensor', 0, 0)  8.6 us
    all_to_all x1, starting transfers between devices, on_device(): terms = lax.all_to_all(terms, 'dp', 0, 0)  7.22 us
    all_to_all x1, starting transfers between devices, on_device(): cp = lax.all_to_all(cp, 'tensor', 0, 0)  5.54 us
  transfers between devices with their start and end apart: 14, of which 13 were waited for; matrix products, arithmetic and copies ran while one was open for 0% of the time, Pallas kernels for 20%

profile of v3, /device:TPU:1, one launch (start us, length us, event | category | flops | bytes accessed | tf_op | source)
XLA Modules:
  0.0 160.4 jit_solution(9642287869226976496)
XLA Ops:
  7.2 0.0 copy-start.5
  7.2 0.0 all-gather.2.cloned.1.call-start
  7.2 0.7 all-gather.2.cloned.1.call-update
  7.9 0.0 copy-start.2
  7.9 2.0 %copy-done.2 = bf16[2048,896]{1,0:T(8,128)(2,1)S(1)} copy-done((bf16[2048,896]{1,0:T(8,128)(2,1)S(1)}, bf16[2048,896]{1,0:T(8,128)(2,1)}, u32[]{:S(2)}) %copy-start.2) | copy-done | bytes 3670040
  9.9 0.0 copy-start.8
  10.0 0.9 copy-done.8
  10.8 2.5 %shard_map.61 = f32[16,32,128]{2,1,0:T(8,128)} custom-call(f32[32,896]{1,0:T(8,128)S(1)} %bitcast.7, bf16[2048,896]{1,0:T(8,128)(2,1)S(1)} %copy-done.2), custom_call_target="tpu_custom_call" | custom-call | flops 1048576 | bytes 65536 | tf_op jit(solution)/shard_map/pallas_call | solution.py:59
  13.4 8.6 %all-to-all-start = ((f32[16,32,128]{2,1,0:T(8,128)}), f32[16,32,128]{2,1,0:T(8,128)S(1)}, u32[]{:S(2)}, u32[]{:S(2)}) async-start(f32[16,32,128]{2,1,0:T(8,128)} %shard_map.61), calls=%async_computation | async-start | bytes 524288 | tf_op jit(solution)/shard_map/all_to_all | solution.py:258
  22.0 0.0 copy-start
  22.0 3.8 %copy-done = bf16[1,4096,896]{2,1,0:T(8,128)(2,1)S(1)} copy-done((bf16[1,4096,896]{2,1,0:T(8,128)(2,1)S(1)}, bf16[1,4096,896]{2,1,0:T(8,128)(2,1)}, u32[]{:S(2)}) %copy-start) | copy-done | bytes 7340056
  25.8 0.0 copy-start.9
  25.8 0.9 copy-done.9
  26.7 3.4 %shard_map.59.refs_1_.refs_2_ = f32[32,4096]{1,0:T(8,128)S(1)} custom-call(f32[32,896]{1,0:T(8,128)S(1)} %bitcast.8, bf16[4096,896]{1,0:T(8,128)(2,1)S(1)} %bitcast.5), custom_call_target="tpu_custom_call" | custom-call | flops 1048576 | bytes 65536 | tf_op jit(solution)/shard_map/pallas_call | solution.py:59
  30.1 0.0 copy-start.6
  30.1 0.0 all-to-all-done.refs_0_
  30.1 0.0 copy-done.5
  30.1 1.4 shard_map.62
  31.5 7.2 %all-to-all-start.1 = ((f32[8,32,512]{2,1,0:T(8,128)}), f32[8,32,512]{2,1,0:T(8,128)S(1)}, u32[]{:S(2)}, u32[]{:S(2)}) async-start(f32[8,32,512]{2,1,0:T(8,128)} %shard_map.62), calls=%async_computation.1 | async-start | bytes 1048576 | tf_op jit(solution)/shard_map/all_to_all | solution.py:276
  38.7 0.0 copy-done.6
  38.7 5.0 %shard_map.60.refs_1_ = bf16[896,2048]{1,0:T(8,128)(2,1)} custom-call(bf16[2048,896]{1,0:T(8,128)(2,1)} %refs_1_.7, f32[32,4096]{1,0:T(8,128)} %copy-done.6), custom_call_target="tpu_custom_call" | custom-call | flops 1048576 | bytes 65536 | tf_op jit(solution)/shard_map/pallas_call | solution.py:59
  43.8 4.4 %all-to-all-done.1.refs_0_ = f32[8,32,512]{2,1,0:T(8,128)S(1)} async-done(((f32[8,32,512]{2,1,0:T(8,128)}), f32[8,32,512]{2,1,0:T(8,128)S(1)}, u32[]{:S(2)}, u32[]{:S(2)}) %all-to-all-start.1) | async-done | bytes 524320 | tf_op jit(solution)/shard_map/all_to_all | solution.py:276
  48.2 0.0 copy-start.4
  48.2 2.0 %copy-done.4 = bf16[896,2048]{1,0:T(8,128)(2,1)S(1)} copy-done((bf16[896,2048]{1,0:T(8,128)(2,1)S(1)}, bf16[896,2048]{1,0:T(8,128)(2,1)}, u32[]{:S(2)}) %copy-start.4) | copy-done | bytes 3670040
  50.3 0.1 collective-permute-start.2
  50.4 2.1 %collective-permute-start.1 = (f32[32,512]{1,0:T(8,128)S(1)}, f32[32,512]{1,0:T(8,128)S(1)}, u32[]{:S(2)}, u32[]{:S(2)}) collective-permute-start(f32[32,512]{1,0:T(8,128)S(1)} %shard_map.63.refs_0_), channel_id=1, source_target_pairs={{2,0},{3,1},{0,2},{1,3},{6,4},{7,5},{4,6},{5,7},{10,8},{11,9},{8,1... | collective-permute-start | bytes 196616 | tf_op jit(solution)/shard_map/ppermute | solution.py:31
  52.5 1.2 collective-permute-start
  53.7 1.6 %collective-permute-done.2.refs_3_ = f32[32,512]{1,0:T(8,128)S(1)} collective-permute-done((f32[32,512]{1,0:T(8,128)S(1)}, f32[32,512]{1,0:T(8,128)S(1)}, u32[]{:S(2)}, u32[]{:S(2)}) %collective-permute-start.2) | collective-permute-done | bytes 65568 | tf_op jit(solution)/shard_map/ppermute | solution.py:31
  55.3 0.1 collective-permute-done.1.refs_2_
  55.4 1.5 collective-permute-done.refs_1_
  57.0 1.0 collective-permute-start.5
  58.0 2.2 %collective-permute-start.4 = (f32[32,512]{1,0:T(8,128)S(1)}, f32[32,512]{1,0:T(8,128)S(1)}, u32[]{:S(2)}, u32[]{:S(2)}) collective-permute-start(f32[32,512]{1,0:T(8,128)S(1)} %shard_map.64.refs_0_), channel_id=1, source_target_pairs={{8,0},{9,1},{10,2},{11,3},{12,4},{13,5},{14,6},{15,7},{0,8},{1,9},... | collective-permute-start | bytes 196616 | tf_op jit(solution)/shard_map/ppermute | solution.py:31
  60.2 1.2 collective-permute-start.3
  61.4 1.7 %collective-permute-done.5.refs_3_ = f32[32,512]{1,0:T(8,128)S(1)} collective-permute-done((f32[32,512]{1,0:T(8,128)S(1)}, f32[32,512]{1,0:T(8,128)S(1)}, u32[]{:S(2)}, u32[]{:S(2)}) %collective-permute-start.5) | collective-permute-done | bytes 65568 | tf_op jit(solution)/shard_map/ppermute | solution.py:31
  63.2 2.6 %collective-permute-done.4.refs_2_ = f32[32,512]{1,0:T(8,128)S(1)} collective-permute-done((f32[32,512]{1,0:T(8,128)S(1)}, f32[32,512]{1,0:T(8,128)S(1)}, u32[]{:S(2)}, u32[]{:S(2)}) %collective-permute-start.4) | collective-permute-done | bytes 65568 | tf_op jit(solution)/shard_map/ppermute | solution.py:31
  65.7 0.1 collective-permute-done.3.refs_1_
  65.9 16.7 %all_to_all.20.refs_0_ = f32[8,32,512]{2,1,0:T(8,128)S(1)} all-to-all(f32[8,32,512]{2,1,0:T(8,128)S(1)} %shard_map.65), channel_id=1, replica_groups=mesh['dp'=8,'tensor'=16] {'dp'}, dimensions={0} | all-to-all | bytes 1048576 | tf_op jit(solution)/shard_map/all_to_all | solution.py:286
  82.6 1.6 shard_map.66
  84.1 5.5 %all-to-all-start.3 = ((f32[16,32,128]{2,1,0:T(8,128)}), f32[16,32,128]{2,1,0:T(8,128)S(1)}, u32[]{:S(2)}, u32[]{:S(2)}) async-start(f32[16,32,128]{2,1,0:T(8,128)} %get-tuple-element.14), calls=%async_computation.3 | async-start | bytes 524288 | tf_op jit(solution)/shard_map/all_to_all | solution.py:293
  89.7 0.0 copy-start.1
  89.7 3.3 %copy-done.1 = bf16[1,4096,896]{2,1,0:T(8,128)(2,1)S(1)} copy-done((bf16[1,4096,896]{2,1,0:T(8,128)(2,1)S(1)}, bf16[1,4096,896]{2,1,0:T(8,128)(2,1)}, u32[]{:S(2)}) %copy-start.1) | copy-done | bytes 7340056
  93.0 6.3 %shard_map.67 = (f32[32,896]{1,0:T(8,128)S(1)}, f32[32,32]{1,0:T(8,128)S(1)}, bf16[192,4096]{1,0:T(8,128)(2,1)S(1)}) custom-call(f32[32,4096]{1,0:T(8,128)S(1)} %get-tuple-element.10.refs_0_, bf16[96,4096]{1,0:T(8,128)(2,1)S(1)} %get-tuple-element.11.refs_1_, bf16[4096,896]{1,0:T(8,128)(2,1)S(1)} %bitcast.6), custom_call_target="tpu_custom_call" | custom-call | flops 1048576 | bytes 65536 | tf_op jit(solution)/shard_map/pallas_call | solution.py:59
  99.4 0.0 copy-start.7
  99.4 1.1 copy-done.7
  100.5 0.3 all-to-all-done.3.refs_0_
  100.8 0.0 copy-start.3
  100.8 2.0 %copy-done.3 = bf16[2048,896]{1,0:T(8,128)(2,1)S(1)} copy-done((bf16[2048,896]{1,0:T(8,128)(2,1)S(1)}, bf16[2048,896]{1,0:T(8,128)(2,1)}, u32[]{:S(2)}) %copy-start.3) | copy-done | bytes 3670040
  102.9 1.2 shard_map.68
  104.1 2.6 %collective-permute-start.6 = (f32[32,896]{1,0:T(8,128)S(1)}, f32[32,896]{1,0:T(8,128)S(1)}, u32[]{:S(2)}, u32[]{:S(2)}) collective-permute-start(f32[32,896]{1,0:T(8,128)S(1)} %shard_map.68), channel_id=1, source_target_pairs={{16,0},{17,1},{18,2},{19,3},{20,4},{21,5},{22,6},{23,7},{24,8},{25... | collective-permute-start | bytes 344072 | tf_op jit(solution)/shard_map/ppermute | solution.py:31
  106.7 1.0 collective-permute-done.6
  107.7 0.4 collective-permute-start.9
  108.1 1.6 %collective-permute-start.8 = (f32[32,896]{1,0:T(8,128)S(1)}, f32[32,896]{1,0:T(8,128)S(1)}, u32[]{:S(2)}, u32[]{:S(2)}) collective-permute-start(f32[32,896]{1,0:T(8,128)S(1)} %add.3.refs_1_), channel_id=1, source_target_pairs={{64,0},{65,1},{66,2},{67,3},{68,4},{69,5},{70,6},{71,7},{72,8},{73... | collective-permute-start | bytes 344072 | tf_op jit(solution)/shard_map/ppermute | solution.py:31
  109.7 0.8 collective-permute-start.7
  110.6 3.6 %collective-permute-done.9.refs_4_ = f32[32,896]{1,0:T(8,128)S(1)} collective-permute-done((f32[32,896]{1,0:T(8,128)S(1)}, f32[32,896]{1,0:T(8,128)S(1)}, u32[]{:S(2)}, u32[]{:S(2)}) %collective-permute-start.9) | collective-permute-done | bytes 114720 | tf_op jit(solution)/shard_map/ppermute | solution.py:31
  114.2 0.9 collective-permute-done.8.refs_3_
  115.1 1.2 collective-permute-done.7.refs_2_
  116.3 0.9 shard_map.69
  117.2 0.0 copy-start.10
  117.2 0.7 copy-done.10
  117.9 10.1 %shard_map.70.refs_2_ = f32[4096,896]{1,0:T(8,128)} custom-call(bf16[192,4096]{1,0:T(8,128)(2,1)} %copy-done.7, bf16[192,896]{1,0:T(8,128)(2,1)} %copy-done.10, bf16[4096,896]{1,0:T(8,128)(2,1)} %bitcast.4), custom_call_target="tpu_custom_call" | custom-call | flops 1048576 | bytes 65536 | tf_op jit(solution)/shard_map/pallas_call | solution.py:59
  128.0 2.8 %all-gather.2.cloned.1.call-done.refs_0_ = bf16[2048,4096]{1,0:T(8,128)(2,1)} async-done(((bf16[128,4096]{1,0:T(8,128)(2,1)}), bf16[2048,4096]{1,0:T(8,128)(2,1)}) %all-gather.2.cloned.1.call-update) | async-done | bytes 16777232 | tf_op jit(solution)/shard_map/all_gather | solution.py:250
  130.9 22.7 %shard_map.71 = bf16[4096,896]{1,0:T(8,128)(2,1)} custom-call(bf16[2048,4096]{1,0:T(8,128)(2,1)} %all-gather.2.cloned.1.call-done.refs_0_, bf16[896,2048]{1,0:T(8,128)(2,1)} %shard_map.60.refs_1_, f32[4096,896]{1,0:T(8,128)} %shard_map.70.refs_2_), custom_call_target="tpu_custom_call" | custom-call | flops 1048576 | bytes 65536 | tf_op jit(solution)/shard_map/pallas_call | solution.py:59
  (4 shorter events, 0.1 us)
Async XLA Ops:
  7.2 22.9 %copy-start.5 = (bf16[128,4096]{1,0:T(8,128)(2,1)S(1)}, bf16[128,4096]{1,0:T(8,128)(2,1)}, u32[]{:S(2)}) copy-start(bf16[128,4096]{1,0:T(8,128)(2,1)} %refs_1_.6) | copy-start | bytes 3145732
  7.2 123.7 %all-gather.2.cloned.1.call-start = ((), (), s32[]{:S(2)}) async-start(), calls=%async_computation.4 | async-start | bytes 17825792 | tf_op jit(solution)/shard_map/all_gather | solution.py:250
  7.9 2.0 %copy-start.2 = (bf16[2048,896]{1,0:T(8,128)(2,1)S(1)}, bf16[2048,896]{1,0:T(8,128)(2,1)}, u32[]{:S(2)}) copy-start(bf16[2048,896]{1,0:T(8,128)(2,1)} %refs_1_.7) | copy-start | bytes 11010052
  9.9 0.9 copy-start.8
  13.4 16.7 %all-to-all-start = ((f32[16,32,128]{2,1,0:T(8,128)}), f32[16,32,128]{2,1,0:T(8,128)S(1)}, u32[]{:S(2)}, u32[]{:S(2)}) async-start(f32[16,32,128]{2,1,0:T(8,128)} %shard_map.61), calls=%async_computation | async-start | bytes 524288 | tf_op jit(solution)/shard_map/all_to_all | solution.py:258
  22.0 3.8 %copy-start = (bf16[1,4096,896]{2,1,0:T(8,128)(2,1)S(1)}, bf16[1,4096,896]{2,1,0:T(8,128)(2,1)}, u32[]{:S(2)}) copy-start(bf16[1,4096,896]{2,1,0:T(8,128)(2,1)} %param.6) | copy-start | bytes 22020100
  25.8 0.9 copy-start.9
  30.1 8.7 %copy-start.6 = (f32[32,4096]{1,0:T(8,128)}, f32[32,4096]{1,0:T(8,128)S(1)}, u32[]{:S(2)}) copy-start(f32[32,4096]{1,0:T(8,128)S(1)} %shard_map.59.refs_1_.refs_2_) | copy-start | bytes 1572868
  31.5 16.7 %all-to-all-start.1 = ((f32[8,32,512]{2,1,0:T(8,128)}), f32[8,32,512]{2,1,0:T(8,128)S(1)}, u32[]{:S(2)}, u32[]{:S(2)}) async-start(f32[8,32,512]{2,1,0:T(8,128)} %shard_map.62), calls=%async_computation.1 | async-start | bytes 1048576 | tf_op jit(solution)/shard_map/all_to_all | solution.py:276
  48.2 2.0 %copy-start.4 = (bf16[896,2048]{1,0:T(8,128)(2,1)S(1)}, bf16[896,2048]{1,0:T(8,128)(2,1)}, u32[]{:S(2)}) copy-start(bf16[896,2048]{1,0:T(8,128)(2,1)} %shard_map.60.refs_1_) | copy-start | bytes 11010052
  50.3 5.0 %collective-permute-start.2 = (f32[32,512]{1,0:T(8,128)S(1)}, f32[32,512]{1,0:T(8,128)S(1)}, u32[]{:S(2)}, u32[]{:S(2)}) collective-permute-start(f32[32,512]{1,0:T(8,128)S(1)} %shard_map.63.refs_0_), channel_id=1, source_target_pairs={{3,0},{0,1},{1,2},{2,3},{7,4},{4,5},{5,6},{6,7},{11,8},{8,9},{9,10... | collective-permute-start | bytes 196616 | tf_op jit(solution)/shard_map/ppermute | solution.py:31
  50.4 5.1 %collective-permute-start.1 = (f32[32,512]{1,0:T(8,128)S(1)}, f32[32,512]{1,0:T(8,128)S(1)}, u32[]{:S(2)}, u32[]{:S(2)}) collective-permute-start(f32[32,512]{1,0:T(8,128)S(1)} %shard_map.63.refs_0_), channel_id=1, source_target_pairs={{2,0},{3,1},{0,2},{1,3},{6,4},{7,5},{4,6},{5,7},{10,8},{11,9},{8,1... | collective-permute-start | bytes 196616 | tf_op jit(solution)/shard_map/ppermute | solution.py:31
  52.5 4.5 %collective-permute-start = (f32[32,512]{1,0:T(8,128)S(1)}, f32[32,512]{1,0:T(8,128)S(1)}, u32[]{:S(2)}, u32[]{:S(2)}) collective-permute-start(f32[32,512]{1,0:T(8,128)S(1)} %shard_map.63.refs_0_), channel_id=1, source_target_pairs={{1,0},{2,1},{3,2},{0,3},{5,4},{6,5},{7,6},{4,7},{9,8},{10,9},{11,1... | collective-permute-start | bytes 196616 | tf_op jit(solution)/shard_map/ppermute | solution.py:31
  57.0 6.2 %collective-permute-start.5 = (f32[32,512]{1,0:T(8,128)S(1)}, f32[32,512]{1,0:T(8,128)S(1)}, u32[]{:S(2)}, u32[]{:S(2)}) collective-permute-start(f32[32,512]{1,0:T(8,128)S(1)} %shard_map.64.refs_0_), channel_id=1, source_target_pairs={{12,0},{13,1},{14,2},{15,3},{0,4},{1,5},{2,6},{3,7},{4,8},{5,9},{6... | collective-permute-start | bytes 196616 | tf_op jit(solution)/shard_map/ppermute | solution.py:31
  58.0 7.8 %collective-permute-start.4 = (f32[32,512]{1,0:T(8,128)S(1)}, f32[32,512]{1,0:T(8,128)S(1)}, u32[]{:S(2)}, u32[]{:S(2)}) collective-permute-start(f32[32,512]{1,0:T(8,128)S(1)} %shard_map.64.refs_0_), channel_id=1, source_target_pairs={{8,0},{9,1},{10,2},{11,3},{12,4},{13,5},{14,6},{15,7},{0,8},{1,9},... | collective-permute-start | bytes 196616 | tf_op jit(solution)/shard_map/ppermute | solution.py:31
  60.2 5.6 %collective-permute-start.3 = (f32[32,512]{1,0:T(8,128)S(1)}, f32[32,512]{1,0:T(8,128)S(1)}, u32[]{:S(2)}, u32[]{:S(2)}) collective-permute-start(f32[32,512]{1,0:T(8,128)S(1)} %shard_map.64.refs_0_), channel_id=1, source_target_pairs={{4,0},{5,1},{6,2},{7,3},{8,4},{9,5},{10,6},{11,7},{12,8},{13,9},{1... | collective-permute-start | bytes 196616 | tf_op jit(solution)/shard_map/ppermute | solution.py:31
  84.1 16.7 %all-to-all-start.3 = ((f32[16,32,128]{2,1,0:T(8,128)}), f32[16,32,128]{2,1,0:T(8,128)S(1)}, u32[]{:S(2)}, u32[]{:S(2)}) async-start(f32[16,32,128]{2,1,0:T(8,128)} %get-tuple-element.14), calls=%async_computation.3 | async-start | bytes 524288 | tf_op jit(solution)/shard_map/all_to_all | solution.py:293
  89.7 3.3 %copy-start.1 = (bf16[1,4096,896]{2,1,0:T(8,128)(2,1)S(1)}, bf16[1,4096,896]{2,1,0:T(8,128)(2,1)}, u32[]{:S(2)}) copy-start(bf16[1,4096,896]{2,1,0:T(8,128)(2,1)} %param.6) | copy-start | bytes 22020100
  99.4 1.1 copy-start.7
  100.8 2.0 %copy-start.3 = (bf16[2048,896]{1,0:T(8,128)(2,1)S(1)}, bf16[2048,896]{1,0:T(8,128)(2,1)}, u32[]{:S(2)}) copy-start(bf16[2048,896]{1,0:T(8,128)(2,1)} %refs_1_.7) | copy-start | bytes 11010052
  104.1 3.6 %collective-permute-start.6 = (f32[32,896]{1,0:T(8,128)S(1)}, f32[32,896]{1,0:T(8,128)S(1)}, u32[]{:S(2)}, u32[]{:S(2)}) collective-permute-start(f32[32,896]{1,0:T(8,128)S(1)} %shard_map.68), channel_id=1, source_target_pairs={{16,0},{17,1},{18,2},{19,3},{20,4},{21,5},{22,6},{23,7},{24,8},{25... | collective-permute-start | bytes 344072 | tf_op jit(solution)/shard_map/ppermute | solution.py:31
  107.7 6.5 %collective-permute-start.9 = (f32[32,896]{1,0:T(8,128)S(1)}, f32[32,896]{1,0:T(8,128)S(1)}, u32[]{:S(2)}, u32[]{:S(2)}) collective-permute-start(f32[32,896]{1,0:T(8,128)S(1)} %add.3.refs_1_), channel_id=1, source_target_pairs={{96,0},{97,1},{98,2},{99,3},{100,4},{101,5},{102,6},{103,7},{104,8... | collective-permute-start | bytes 344072 | tf_op jit(solution)/shard_map/ppermute | solution.py:31
  108.1 7.0 %collective-permute-start.8 = (f32[32,896]{1,0:T(8,128)S(1)}, f32[32,896]{1,0:T(8,128)S(1)}, u32[]{:S(2)}, u32[]{:S(2)}) collective-permute-start(f32[32,896]{1,0:T(8,128)S(1)} %add.3.refs_1_), channel_id=1, source_target_pairs={{64,0},{65,1},{66,2},{67,3},{68,4},{69,5},{70,6},{71,7},{72,8},{73... | collective-permute-start | bytes 344072 | tf_op jit(solution)/shard_map/ppermute | solution.py:31
  109.7 6.5 %collective-permute-start.7 = (f32[32,896]{1,0:T(8,128)S(1)}, f32[32,896]{1,0:T(8,128)S(1)}, u32[]{:S(2)}, u32[]{:S(2)}) collective-permute-start(f32[32,896]{1,0:T(8,128)S(1)} %add.3.refs_1_), channel_id=1, source_target_pairs={{32,0},{33,1},{34,2},{35,3},{36,4},{37,5},{38,6},{39,7},{40,8},{41... | collective-permute-start | bytes 344072 | tf_op jit(solution)/shard_map/ppermute | solution.py:31
  117.2 0.7 copy-start.10
Sparse Core Ops, SparseCore 0:
  10.1 120.6 all-gather.1

commit v4 on v2

--- a/solution.py
+++ b/solution.py
@@ -127,16 +127,21 @@
     refs[-1][...] = total
 
 
-def sum_copies_body(*refs):
-    total = (refs[0][...] + refs[1][...]) + (refs[2][...] + refs[3][...])
-    refs[4][...] = jnp.broadcast_to(total[None], refs[4].shape)
-
-
-def sum_pieces_body(pieces, out):
+def place_copies_body(pos, *refs):
+    out = refs[4]
+    for k in range(4):
+        out[:, (pos[0] + k) % 4] = jnp.broadcast_to(refs[k][...][None], (N_DP, RANK, TOK))
+
+
+def sum_pieces_body(pos, pieces, *outs):
     total = pieces[0]
     for r in range(1, N_DP):
         total += pieces[r]
-    out[...] = total
+    quarters = outs[4]
+    for k in range(4):
+        quarters[k] = total[:, k * TOK:(k + 1) * TOK]
+    for k in range(4):
+        outs[k][...] = quarters[(pos[0] + 4 - k) % 4]
 
 
 def cp_body(power_pieces, c, power, pieces, out, acc):
@@ -146,7 +151,9 @@
     def _():
         acc[...] = jnp.zeros_like(acc)
 
-    block = jnp.concatenate([power_pieces[j] for j in range(power_pieces.shape[0])], axis=1)
+    block = jnp.concatenate(
+        [power_pieces[j, k] for j in range(power_pieces.shape[0]) for k in range(4)], axis=1
+    )
     power[...] = block
     split = split3(block)
     pieces[...] = split
@@ -271,14 +278,21 @@
         scratch=[pltpu.VMEM((3 * RANK, TOK), BF16)],
     )
     terms = lax.all_to_all(terms, "dp", 0, 0)
-    (piece,) = kernel_call(sum_pieces_body, 1, [terms], [None], [f32(RANK, BLOCK)], [None])
-    (piece,) = kernel_call(sum_body, 1, around([piece] * 4, "y"), [None] * 4, [f32(RANK, BLOCK)], [None])
+    pos = jnp.reshape(lax.axis_index("tensor") % NY, (1,)).astype(jnp.int32)
+    quarter = f32(RANK, TOK)
+    sends = kernel_call(
+        sum_pieces_body, 1, [pos, terms], [SMEM, None], [quarter] * 4, [None] * 4,
+        scratch=[pltpu.VMEM((4, RANK, TOK), F32)],
+    )
+    (piece,) = kernel_call(sum_body, 1, around(sends, "y"), [None] * 4, [quarter], [None])
+    (piece,) = kernel_call(sum_body, 1, around([piece] * 4, "z"), [None] * 4, [quarter], [None])
     (copies,) = kernel_call(
-        sum_copies_body, 1, around([piece] * 4, "z"), [None] * 4, [f32(N_DP, RANK, BLOCK)], [None],
+        place_copies_body, 1, [pos, *around([piece] * 4, "y")], [SMEM] + [None] * 4, [f32(N_DP, 4, RANK, TOK)], [None],
     )
     power_pieces = lax.all_to_all(copies, "dp", 0, 0)
     power, pieces, cp = kernel_call(
-        cp_body, 2, [power_pieces, cotangent], [piece_spec, c_spec],
+        cp_body, 2, [power_pieces, cotangent],
+        [pl.BlockSpec((wide, 4, RANK, TOK), lambda i: (i, 0, 0, 0)), c_spec],
         [f32(RANK, rows), bf16(3 * RANK, rows), f32(NZ * NY, RANK, TOK)],
         [wide_spec, pl.BlockSpec((3 * RANK, wide * BLOCK), lambda i: (0, i)), None],
         scratch=[pltpu.VMEM((RANK, TOK), F32)],

time: 162 us -> 160 us (0.988)
  blocking collectives: 31.4 us -> 16.7 us
  starting transfers between devices: 28.8 us -> 37.4 us
  waiting for transfers between devices: 21.4 us -> 25 us
    all_to_all x1 -> x0, blocking collectives: 16.4 us -> none  [on_device(): terms = lax.all_to_all(terms, 'dp', 0, 0)]
    all_to_all x0 -> x1, waiting for transfers between devices: none -> 9.48 us  [on_device(): terms = lax.all_to_all(terms, 'dp', 0, 0)]
    all_to_all x0 -> x1, starting transfers between devices: none -> 7.21 us  [on_device(): terms = lax.all_to_all(terms, 'dp', 0, 0)]
    all_gather x1, waiting for transfers between devices: 6.88 us -> 0.25 us  [on_device(): gathered = lax.all_gather(cotangent, 'tensor', axis=0, tiled=True)]
    all_to_all x1, blocking collectives: 15 us -> 16.7 us  [on_device(): power_pieces = lax.all_to_all(copies, 'dp', 0, 0)]
    ppermute x10 -> x13, starting transfers between devices: 14 us -> 15.6 us  [fetch(): return lax.ppermute(array, AXES, receive_from(**offsets))]
    ppermute x10 -> x13, waiting for transfers between devices: 13.3 us -> 14.1 us  [fetch(): return lax.ppermute(array, AXES, receive_from(**offsets))]
    pallas_call x12 -> x13, Pallas kernels: 50.4 us -> 51.1 us  [kernel_call(): pl.pallas_call(call, grid=(grid,), in_specs=[whole(a) if s is None else s...]
  transfers between devices with their start and end apart: 13 -> 17, of which waited for: 10 -> 14; matrix products, arithmetic and copies ran while one was open for 0% -> 0% of each run, Pallas kernels for 17% -> 17%
where the time goes in v4:
time: 160 us; the launch traced here: 159 us
  Pallas kernels  51.1 us (32%)
  starting transfers between devices  37.4 us (23%)
  waiting for transfers between devices  25 us (16%)
  blocking collectives  16.7 us (10%)
  local copies, waits for them, and re-layouts  14.8 us (9%)
  between operations  14.2 us (9%)
    pallas_call x13, Pallas kernels, kernel_call(): pl.pallas_call(call, grid=(grid,), in_specs=[whole(a) if s is None else s...  51.1 us
    all_to_all x1, blocking collectives, on_device(): power_pieces = lax.all_to_all(copies, 'dp', 0, 0)  16.7 us
    ppermute x13, starting transfers between devices, fetch(): return lax.ppermute(array, AXES, receive_from(**offsets))  15.6 us
    unnamed x18, local copies, waits for them, and re-layouts  14.8 us
    ppermute x13, waiting for transfers between devices, fetch(): return lax.ppermute(array, AXES, receive_from(**offsets))  14.1 us
    all_to_all x1, waiting for transfers between devices, on_device(): terms = lax.all_to_all(terms, 'dp', 0, 0)  9.48 us
    all_to_all x1, starting transfers between devices, on_device(): hq = lax.all_to_all(hq, 'tensor', 0, 0)  8.59 us
    all_to_all x1, starting transfers between devices, on_device(): terms = lax.all_to_all(terms, 'dp', 0, 0)  7.21 us
  transfers between devices with their start and end apart: 17, of which 14 were waited for; matrix products, arithmetic and copies ran while one was open for 0% of the time, Pallas kernels for 17%

profile of v4, /device:TPU:1, one launch (start us, length us, event | category | flops | bytes accessed | tf_op | source)
XLA Modules:
  0.0 159.1 jit_solution(6139243490585652448)
XLA Ops:
  7.2 0.0 copy-start.4
  7.2 0.0 all-gather.2.cloned.1.call-start
  7.2 0.7 all-gather.2.cloned.1.call-update
  7.9 0.0 copy-start.2
  7.9 2.0 %copy-done.2 = bf16[2048,896]{1,0:T(8,128)(2,1)S(1)} copy-done((bf16[2048,896]{1,0:T(8,128)(2,1)S(1)}, bf16[2048,896]{1,0:T(8,128)(2,1)}, u32[]{:S(2)}) %copy-start.2) | copy-done | bytes 3670040
  9.9 0.0 copy-start.6
  10.0 0.9 copy-done.6
  10.8 2.5 %shard_map.59 = f32[16,32,128]{2,1,0:T(8,128)} custom-call(f32[32,896]{1,0:T(8,128)S(1)} %bitcast.8, bf16[2048,896]{1,0:T(8,128)(2,1)S(1)} %copy-done.2), custom_call_target="tpu_custom_call" | custom-call | flops 1048576 | bytes 65536 | tf_op jit(solution)/shard_map/pallas_call | solution.py:59
  13.4 8.6 %all-to-all-start = ((f32[16,32,128]{2,1,0:T(8,128)}), f32[16,32,128]{2,1,0:T(8,128)S(1)}, u32[]{:S(2)}, u32[]{:S(2)}) async-start(f32[16,32,128]{2,1,0:T(8,128)} %shard_map.59), calls=%async_computation | async-start | bytes 524288 | tf_op jit(solution)/shard_map/all_to_all | solution.py:262
  22.0 0.0 copy-start
  22.0 3.8 %copy-done = bf16[1,4096,896]{2,1,0:T(8,128)(2,1)S(1)} copy-done((bf16[1,4096,896]{2,1,0:T(8,128)(2,1)S(1)}, bf16[1,4096,896]{2,1,0:T(8,128)(2,1)}, u32[]{:S(2)}) %copy-start) | copy-done | bytes 7340056
  25.8 0.0 copy-start.7
  25.8 0.9 copy-done.7
  26.7 3.4 %shard_map.60.refs_2_ = f32[32,4096]{1,0:T(8,128)S(1)} custom-call(f32[32,896]{1,0:T(8,128)S(1)} %bitcast.9, bf16[4096,896]{1,0:T(8,128)(2,1)S(1)} %bitcast.6), custom_call_target="tpu_custom_call" | custom-call | flops 1048576 | bytes 65536 | tf_op jit(solution)/shard_map/pallas_call | solution.py:59
  30.1 0.0 all-to-all-done.refs_0_
  30.1 0.0 copy-done.4
  30.1 1.4 shard_map.61
  31.5 7.2 %all-to-all-start.1 = ((f32[8,32,512]{2,1,0:T(8,128)}), f32[8,32,512]{2,1,0:T(8,128)S(1)}, u32[]{:S(2)}, u32[]{:S(2)}) async-start(f32[8,32,512]{2,1,0:T(8,128)} %shard_map.61), calls=%async_computation.1 | async-start | bytes 1048576 | tf_op jit(solution)/shard_map/all_to_all | solution.py:280
  38.7 9.5 %all-to-all-done.1.refs_1_ = f32[8,32,512]{2,1,0:T(8,128)S(1)} async-done(((f32[8,32,512]{2,1,0:T(8,128)}), f32[8,32,512]{2,1,0:T(8,128)S(1)}, u32[]{:S(2)}, u32[]{:S(2)}) %all-to-all-start.1) | async-done | bytes 524320 | tf_op jit(solution)/shard_map/all_to_all | solution.py:280
  48.2 1.0 collective-permute-start
  49.3 0.6 collective-permute-start.1
  49.8 0.6 collective-permute-start.2
  50.4 0.5 collective-permute-done.refs_1_
  50.9 2.5 %collective-permute-done.1.refs_2_ = f32[32,128]{1,0:T(8,128)S(1)} collective-permute-done((f32[32,128]{1,0:T(8,128)S(1)}, f32[32,128]{1,0:T(8,128)S(1)}, u32[]{:S(2)}, u32[]{:S(2)}) %collective-permute-start.1) | collective-permute-done | bytes 16416 | tf_op jit(solution)/shard_map/ppermute | solution.py:31
  53.4 0.3 collective-permute-done.2.refs_3_
  53.6 1.2 collective-permute-start.5
  54.8 2.4 %collective-permute-start.4 = (f32[32,128]{1,0:T(8,128)S(1)}, f32[32,128]{1,0:T(8,128)S(1)}, u32[]{:S(2)}, u32[]{:S(2)}) collective-permute-start(f32[32,128]{1,0:T(8,128)S(1)} %shard_map.63.refs_0_), channel_id=1, source_target_pairs={{8,0},{9,1},{10,2},{11,3},{12,4},{13,5},{14,6},{15,7},{0,8},{1,9},... | collective-permute-start | bytes 49160 | tf_op jit(solution)/shard_map/ppermute | solution.py:31
  57.2 1.2 collective-permute-start.3
  58.4 0.0 collective-permute-done.5.refs_3_
  58.4 0.7 collective-permute-done.4.refs_2_
  59.1 1.4 collective-permute-done.3.refs_1_
  60.5 0.0 collective-permute-start.8
  60.5 1.6 collective-permute-start.7
  62.1 1.7 %collective-permute-start.6 = (f32[32,128]{1,0:T(8,128)S(1)}, f32[32,128]{1,0:T(8,128)S(1)}, u32[]{:S(2)}, u32[]{:S(2)}) collective-permute-start(f32[32,128]{1,0:T(8,128)S(1)} %shard_map.64.refs_1_), channel_id=1, source_target_pairs={{1,0},{2,1},{3,2},{0,3},{5,4},{6,5},{7,6},{4,7},{9,8},{10,9},{11,1... | collective-permute-start | bytes 49160 | tf_op jit(solution)/shard_map/ppermute | solution.py:31
  63.8 1.3 collective-permute-done.8.refs_4_
  65.1 0.0 collective-permute-done.7.refs_3_
  65.1 1.0 collective-permute-done.6.refs_2_
  66.2 16.7 %all_to_all.20.refs_0_ = f32[8,4,32,128]{3,2,1,0:T(8,128)S(1)} all-to-all(f32[8,4,32,128]{3,2,1,0:T(8,128)S(1)} %shard_map.65), channel_id=1, replica_groups=mesh['dp'=8,'tensor'=16] {'dp'}, dimensions={0} | all-to-all | bytes 1048576 | tf_op jit(solution)/shard_map/all_to_all | solution.py:292
  82.9 1.5 shard_map.66
  84.5 5.9 %all-to-all-start.3 = ((f32[16,32,128]{2,1,0:T(8,128)}), f32[16,32,128]{2,1,0:T(8,128)S(1)}, u32[]{:S(2)}, u32[]{:S(2)}) async-start(f32[16,32,128]{2,1,0:T(8,128)} %get-tuple-element.22), calls=%async_computation.3 | async-start | bytes 524288 | tf_op jit(solution)/shard_map/all_to_all | solution.py:300
  90.4 0.0 copy-start.1
  90.4 3.1 %copy-done.1 = bf16[1,4096,896]{2,1,0:T(8,128)(2,1)S(1)} copy-done((bf16[1,4096,896]{2,1,0:T(8,128)(2,1)S(1)}, bf16[1,4096,896]{2,1,0:T(8,128)(2,1)}, u32[]{:S(2)}) %copy-start.1) | copy-done | bytes 7340056
  93.5 6.4 %shard_map.67 = (f32[32,896]{1,0:T(8,128)S(1)}, f32[32,32]{1,0:T(8,128)S(1)}, bf16[192,4096]{1,0:T(8,128)(2,1)S(1)}) custom-call(f32[32,4096]{1,0:T(8,128)S(1)} %get-tuple-element.18.refs_0_, bf16[96,4096]{1,0:T(8,128)(2,1)S(1)} %get-tuple-element.19.refs_1_, bf16[4096,896]{1,0:T(8,128)(2,1)S(1)} %bitcast.7), custom_call_target="tpu_custom_call" | custom-call | flops 1048576 | bytes 65536 | tf_op jit(solution)/shard_map/pallas_call | solution.py:59
  99.9 0.0 copy-start.5
  99.9 1.1 copy-done.5
  101.0 0.5 all-to-all-done.3.refs_0_
  101.6 0.0 copy-start.3
  101.6 2.2 %copy-done.3 = bf16[2048,896]{1,0:T(8,128)(2,1)S(1)} copy-done((bf16[2048,896]{1,0:T(8,128)(2,1)S(1)}, bf16[2048,896]{1,0:T(8,128)(2,1)}, u32[]{:S(2)}) %copy-start.3) | copy-done | bytes 3670040
  103.7 1.2 shard_map.68
  105.0 2.3 %collective-permute-start.9 = (f32[32,896]{1,0:T(8,128)S(1)}, f32[32,896]{1,0:T(8,128)S(1)}, u32[]{:S(2)}, u32[]{:S(2)}) collective-permute-start(f32[32,896]{1,0:T(8,128)S(1)} %shard_map.68), channel_id=1, source_target_pairs={{16,0},{17,1},{18,2},{19,3},{20,4},{21,5},{22,6},{23,7},{24,8},{25... | collective-permute-start | bytes 344072 | tf_op jit(solution)/shard_map/ppermute | solution.py:31
  107.3 1.0 collective-permute-done.9
  108.3 0.6 collective-permute-start.12
  108.9 1.7 %collective-permute-start.11 = (f32[32,896]{1,0:T(8,128)S(1)}, f32[32,896]{1,0:T(8,128)S(1)}, u32[]{:S(2)}, u32[]{:S(2)}) collective-permute-start(f32[32,896]{1,0:T(8,128)S(1)} %add.8.refs_1_), channel_id=1, source_target_pairs={{64,0},{65,1},{66,2},{67,3},{68,4},{69,5},{70,6},{71,7},{72,8},{73... | collective-permute-start | bytes 344072 | tf_op jit(solution)/shard_map/ppermute | solution.py:31
  110.6 0.8 collective-permute-start.10
  111.4 3.1 %collective-permute-done.12.refs_4_ = f32[32,896]{1,0:T(8,128)S(1)} collective-permute-done((f32[32,896]{1,0:T(8,128)S(1)}, f32[32,896]{1,0:T(8,128)S(1)}, u32[]{:S(2)}, u32[]{:S(2)}) %collective-permute-start.12) | collective-permute-done | bytes 114720 | tf_op jit(solution)/shard_map/ppermute | solution.py:31
  114.5 1.5 collective-permute-done.11.refs_3_
  116.0 0.8 collective-permute-done.10.refs_2_
  116.8 0.9 shard_map.69
  117.7 0.0 copy-start.8
  117.7 0.7 copy-done.8
  118.4 10.1 %shard_map.70.refs_2_ = f32[4096,896]{1,0:T(8,128)} custom-call(bf16[192,4096]{1,0:T(8,128)(2,1)} %copy-done.5, bf16[192,896]{1,0:T(8,128)(2,1)} %copy-done.8, bf16[4096,896]{1,0:T(8,128)(2,1)} %bitcast.5), custom_call_target="tpu_custom_call" | custom-call | flops 1048576 | bytes 65536 | tf_op jit(solution)/shard_map/pallas_call | solution.py:59
  128.5 0.2 all-gather.2.cloned.1.call-done.refs_0_
  128.8 23.5 %shard_map.71 = bf16[4096,896]{1,0:T(8,128)(2,1)} custom-call(bf16[2048,4096]{1,0:T(8,128)(2,1)} %all-gather.2.cloned.1.call-done.refs_0_, bf16[2048,896]{1,0:T(8,128)(2,1)} %refs_1_.9, f32[4096,896]{1,0:T(8,128)} %shard_map.70.refs_2_), custom_call_target="tpu_custom_call" | custom-call | flops 1048576 | bytes 65536 | tf_op jit(solution)/shard_map/pallas_call | solution.py:59
  (5 shorter events, 0.1 us)
Async XLA Ops:
  7.2 22.9 %copy-start.4 = (bf16[128,4096]{1,0:T(8,128)(2,1)S(1)}, bf16[128,4096]{1,0:T(8,128)(2,1)}, u32[]{:S(2)}) copy-start(bf16[128,4096]{1,0:T(8,128)(2,1)} %refs_1_.7) | copy-start | bytes 3145732
  7.2 121.6 %all-gather.2.cloned.1.call-start = ((), (), s32[]{:S(2)}) async-start(), calls=%async_computation.4 | async-start | bytes 17825792 | tf_op jit(solution)/shard_map/all_gather | solution.py:254
  7.9 2.0 %copy-start.2 = (bf16[2048,896]{1,0:T(8,128)(2,1)S(1)}, bf16[2048,896]{1,0:T(8,128)(2,1)}, u32[]{:S(2)}) copy-start(bf16[2048,896]{1,0:T(8,128)(2,1)} %refs_1_.9) | copy-start | bytes 11010052
  9.9 0.9 copy-start.6
  13.4 16.7 %all-to-all-start = ((f32[16,32,128]{2,1,0:T(8,128)}), f32[16,32,128]{2,1,0:T(8,128)S(1)}, u32[]{:S(2)}, u32[]{:S(2)}) async-start(f32[16,32,128]{2,1,0:T(8,128)} %shard_map.59), calls=%async_computation | async-start | bytes 524288 | tf_op jit(solution)/shard_map/all_to_all | solution.py:262
  22.0 3.8 %copy-start = (bf16[1,4096,896]{2,1,0:T(8,128)(2,1)S(1)}, bf16[1,4096,896]{2,1,0:T(8,128)(2,1)}, u32[]{:S(2)}) copy-start(bf16[1,4096,896]{2,1,0:T(8,128)(2,1)} %param.6) | copy-start | bytes 22020100
  25.8 0.9 copy-start.7
  31.5 16.7 %all-to-all-start.1 = ((f32[8,32,512]{2,1,0:T(8,128)}), f32[8,32,512]{2,1,0:T(8,128)S(1)}, u32[]{:S(2)}, u32[]{:S(2)}) async-start(f32[8,32,512]{2,1,0:T(8,128)} %shard_map.61), calls=%async_computation.1 | async-start | bytes 1048576 | tf_op jit(solution)/shard_map/all_to_all | solution.py:280
  48.2 2.7 %collective-permute-start = (f32[32,128]{1,0:T(8,128)S(1)}, f32[32,128]{1,0:T(8,128)S(1)}, u32[]{:S(2)}, u32[]{:S(2)}) collective-permute-start(f32[32,128]{1,0:T(8,128)S(1)} %get-tuple-element.15), channel_id=1, source_target_pairs={{1,0},{2,1},{3,2},{0,3},{5,4},{6,5},{7,6},{4,7},{9,8},{10,9},{11,1... | collective-permute-start | bytes 49160 | tf_op jit(solution)/shard_map/ppermute | solution.py:31
  49.3 4.1 %collective-permute-start.1 = (f32[32,128]{1,0:T(8,128)S(1)}, f32[32,128]{1,0:T(8,128)S(1)}, u32[]{:S(2)}, u32[]{:S(2)}) collective-permute-start(f32[32,128]{1,0:T(8,128)S(1)} %get-tuple-element.16), channel_id=1, source_target_pairs={{2,0},{3,1},{0,2},{1,3},{6,4},{7,5},{4,6},{5,7},{10,8},{11,9},{8,1... | collective-permute-start | bytes 49160 | tf_op jit(solution)/shard_map/ppermute | solution.py:31
  49.8 3.8 %collective-permute-start.2 = (f32[32,128]{1,0:T(8,128)S(1)}, f32[32,128]{1,0:T(8,128)S(1)}, u32[]{:S(2)}, u32[]{:S(2)}) collective-permute-start(f32[32,128]{1,0:T(8,128)S(1)} %get-tuple-element.17), channel_id=1, source_target_pairs={{3,0},{0,1},{1,2},{2,3},{7,4},{4,5},{5,6},{6,7},{11,8},{8,9},{9,10... | collective-permute-start | bytes 49160 | tf_op jit(solution)/shard_map/ppermute | solution.py:31
  53.6 4.8 %collective-permute-start.5 = (f32[32,128]{1,0:T(8,128)S(1)}, f32[32,128]{1,0:T(8,128)S(1)}, u32[]{:S(2)}, u32[]{:S(2)}) collective-permute-start(f32[32,128]{1,0:T(8,128)S(1)} %shard_map.63.refs_0_), channel_id=1, source_target_pairs={{12,0},{13,1},{14,2},{15,3},{0,4},{1,5},{2,6},{3,7},{4,8},{5,9},{6... | collective-permute-start | bytes 49160 | tf_op jit(solution)/shard_map/ppermute | solution.py:31
  54.8 4.2 %collective-permute-start.4 = (f32[32,128]{1,0:T(8,128)S(1)}, f32[32,128]{1,0:T(8,128)S(1)}, u32[]{:S(2)}, u32[]{:S(2)}) collective-permute-start(f32[32,128]{1,0:T(8,128)S(1)} %shard_map.63.refs_0_), channel_id=1, source_target_pairs={{8,0},{9,1},{10,2},{11,3},{12,4},{13,5},{14,6},{15,7},{0,8},{1,9},... | collective-permute-start | bytes 49160 | tf_op jit(solution)/shard_map/ppermute | solution.py:31
  57.2 3.3 %collective-permute-start.3 = (f32[32,128]{1,0:T(8,128)S(1)}, f32[32,128]{1,0:T(8,128)S(1)}, u32[]{:S(2)}, u32[]{:S(2)}) collective-permute-start(f32[32,128]{1,0:T(8,128)S(1)} %shard_map.63.refs_0_), channel_id=1, source_target_pairs={{4,0},{5,1},{6,2},{7,3},{8,4},{9,5},{10,6},{11,7},{12,8},{13,9},{1... | collective-permute-start | bytes 49160 | tf_op jit(solution)/shard_map/ppermute | solution.py:31
  60.5 4.6 %collective-permute-start.8 = (f32[32,128]{1,0:T(8,128)S(1)}, f32[32,128]{1,0:T(8,128)S(1)}, u32[]{:S(2)}, u32[]{:S(2)}) collective-permute-start(f32[32,128]{1,0:T(8,128)S(1)} %shard_map.64.refs_1_), channel_id=1, source_target_pairs={{3,0},{0,1},{1,2},{2,3},{7,4},{4,5},{5,6},{6,7},{11,8},{8,9},{9,10... | collective-permute-start | bytes 49160 | tf_op jit(solution)/shard_map/ppermute | solution.py:31
  60.5 4.6 %collective-permute-start.7 = (f32[32,128]{1,0:T(8,128)S(1)}, f32[32,128]{1,0:T(8,128)S(1)}, u32[]{:S(2)}, u32[]{:S(2)}) collective-permute-start(f32[32,128]{1,0:T(8,128)S(1)} %shard_map.64.refs_1_), channel_id=1, source_target_pairs={{2,0},{3,1},{0,2},{1,3},{6,4},{7,5},{4,6},{5,7},{10,8},{11,9},{8,1... | collective-permute-start | bytes 49160 | tf_op jit(solution)/shard_map/ppermute | solution.py:31
  62.1 4.1 %collective-permute-start.6 = (f32[32,128]{1,0:T(8,128)S(1)}, f32[32,128]{1,0:T(8,128)S(1)}, u32[]{:S(2)}, u32[]{:S(2)}) collective-permute-start(f32[32,128]{1,0:T(8,128)S(1)} %shard_map.64.refs_1_), channel_id=1, source_target_pairs={{1,0},{2,1},{3,2},{0,3},{5,4},{6,5},{7,6},{4,7},{9,8},{10,9},{11,1... | collective-permute-start | bytes 49160 | tf_op jit(solution)/shard_map/ppermute | solution.py:31
  84.5 17.1 %all-to-all-start.3 = ((f32[16,32,128]{2,1,0:T(8,128)}), f32[16,32,128]{2,1,0:T(8,128)S(1)}, u32[]{:S(2)}, u32[]{:S(2)}) async-start(f32[16,32,128]{2,1,0:T(8,128)} %get-tuple-element.22), calls=%async_computation.3 | async-start | bytes 524288 | tf_op jit(solution)/shard_map/all_to_all | solution.py:300
  90.4 3.1 %copy-start.1 = (bf16[1,4096,896]{2,1,0:T(8,128)(2,1)S(1)}, bf16[1,4096,896]{2,1,0:T(8,128)(2,1)}, u32[]{:S(2)}) copy-start(bf16[1,4096,896]{2,1,0:T(8,128)(2,1)} %param.6) | copy-start | bytes 22020100
  99.9 1.1 copy-start.5
  101.6 2.2 %copy-start.3 = (bf16[2048,896]{1,0:T(8,128)(2,1)S(1)}, bf16[2048,896]{1,0:T(8,128)(2,1)}, u32[]{:S(2)}) copy-start(bf16[2048,896]{1,0:T(8,128)(2,1)} %refs_1_.9) | copy-start | bytes 11010052
  105.0 3.3 %collective-permute-start.9 = (f32[32,896]{1,0:T(8,128)S(1)}, f32[32,896]{1,0:T(8,128)S(1)}, u32[]{:S(2)}, u32[]{:S(2)}) collective-permute-start(f32[32,896]{1,0:T(8,128)S(1)} %shard_map.68), channel_id=1, source_target_pairs={{16,0},{17,1},{18,2},{19,3},{20,4},{21,5},{22,6},{23,7},{24,8},{25... | collective-permute-start | bytes 344072 | tf_op jit(solution)/shard_map/ppermute | solution.py:31
  108.3 6.2 %collective-permute-start.12 = (f32[32,896]{1,0:T(8,128)S(1)}, f32[32,896]{1,0:T(8,128)S(1)}, u32[]{:S(2)}, u32[]{:S(2)}) collective-permute-start(f32[32,896]{1,0:T(8,128)S(1)} %add.8.refs_1_), channel_id=1, source_target_pairs={{96,0},{97,1},{98,2},{99,3},{100,4},{101,5},{102,6},{103,7},{104,8... | collective-permute-start | bytes 344072 | tf_op jit(solution)/shard_map/ppermute | solution.py:31
  108.9 7.1 %collective-permute-start.11 = (f32[32,896]{1,0:T(8,128)S(1)}, f32[32,896]{1,0:T(8,128)S(1)}, u32[]{:S(2)}, u32[]{:S(2)}) collective-permute-start(f32[32,896]{1,0:T(8,128)S(1)} %add.8.refs_1_), channel_id=1, source_target_pairs={{64,0},{65,1},{66,2},{67,3},{68,4},{69,5},{70,6},{71,7},{72,8},{73... | collective-permute-start | bytes 344072 | tf_op jit(solution)/shard_map/ppermute | solution.py:31
  110.6 6.2 %collective-permute-start.10 = (f32[32,896]{1,0:T(8,128)S(1)}, f32[32,896]{1,0:T(8,128)S(1)}, u32[]{:S(2)}, u32[]{:S(2)}) collective-permute-start(f32[32,896]{1,0:T(8,128)S(1)} %add.8.refs_1_), channel_id=1, source_target_pairs={{32,0},{33,1},{34,2},{35,3},{36,4},{37,5},{38,6},{39,7},{40,8},{41... | collective-permute-start | bytes 344072 | tf_op jit(solution)/shard_map/ppermute | solution.py:31
  117.7 0.7 copy-start.8
Sparse Core Ops, SparseCore 0:
  10.1 118.5 all-gather.1

commit v5 on v4

--- a/solution.py
+++ b/solution.py
@@ -224,12 +224,16 @@
     out[...] = e[...].astype(F32) - update
 
 
-def error_body(c, h, rest, out):
-    gradient = lax.dot_general(c[...], h[...], (((0,), (0,)), ((), ())), preferred_element_type=F32)
-    out[...] = (gradient + rest[...]).astype(BF16)
-
-
-def error_calls(gathered, h, basis, q, e):
+def turn_body(h, out):
+    out[...] = h[...].T
+
+
+def error_body(c, h_t, rest, out):
+    gradient = dot_nn(h_t[...], c[...])
+    out[...] = (gradient.T + rest[...]).astype(BF16)
+
+
+def error_calls(gathered, h_t, basis, q, e):
     rows, columns = e.shape
     wide = 2 * BLOCK
     in_rows = pl.BlockSpec((wide, columns), lambda i: (i, 0))
@@ -237,10 +241,9 @@
         rest_body, rows // wide, [basis, q, e],
         [pl.BlockSpec((basis.shape[0], wide), lambda i: (0, i)), None, in_rows], [f32(rows, columns)], [in_rows], vmem_mib=56,
     )
-    in_rows = pl.BlockSpec((BLOCK, columns), lambda i: (i, 0))
     return kernel_call(
-        error_body, rows // BLOCK, [gathered, h, rest],
-        [pl.BlockSpec((gathered.shape[0], BLOCK), lambda i: (0, i)), None, in_rows],
+        error_body, rows // wide, [gathered, h_t, rest],
+        [pl.BlockSpec((gathered.shape[0], wide), lambda i: (0, i)), None, in_rows],
         [bf16(rows, columns)], [in_rows], vmem_mib=56,
     )[0]
 
@@ -289,13 +292,17 @@
     (copies,) = kernel_call(
         place_copies_body, 1, [pos, *around([piece] * 4, "y")], [SMEM] + [None] * 4, [f32(N_DP, 4, RANK, TOK)], [None],
     )
+    (hidden_t,) = kernel_call(
+        turn_body, NZ, [hidden], [pl.BlockSpec((4 * TOK, columns), lambda i: (i, 0))], [bf16(columns, hidden.shape[0])],
+        [pl.BlockSpec((columns, 4 * TOK), lambda i: (0, i))], vmem_mib=56, after=[copies],
+    )
     power_pieces = lax.all_to_all(copies, "dp", 0, 0)
     power, pieces, cp = kernel_call(
         cp_body, 2, [power_pieces, cotangent],
         [pl.BlockSpec((wide, 4, RANK, TOK), lambda i: (i, 0, 0, 0)), c_spec],
         [f32(RANK, rows), bf16(3 * RANK, rows), f32(NZ * NY, RANK, TOK)],
         [wide_spec, pl.BlockSpec((3 * RANK, wide * BLOCK), lambda i: (0, i)), None],
-        scratch=[pltpu.VMEM((RANK, TOK), F32)],
+        scratch=[pltpu.VMEM((RANK, TOK), F32)], after=[hidden_t],
     )
     cp = lax.all_to_all(cp, "tensor", 0, 0)
     ep, inverse, basis = kernel_call(
@@ -315,7 +322,7 @@
         [f32(RANK, columns), bf16(6 * RANK, columns)], [None] * 2,
     )
 
-    out = error_calls(gathered, hidden, basis, q_pieces, error)
+    out = error_calls(gathered, hidden_t, basis, q_pieces, error)
     return out[None], q_mean.T
 
 

time: 160 us -> 163 us (1.019)
  blocking collectives: 16.7 us -> 0 us
  starting transfers between devices: 37.4 us -> 45.7 us
  Pallas kernels: 51.1 us -> 56.1 us
  waiting for transfers between devices: 25 us -> 29.6 us
  local copies, waits for them, and re-layouts: 14.8 us -> 16.9 us
    all_to_all x1 -> x0, blocking collectives: 16.7 us -> none  [on_device(): power_pieces = lax.all_to_all(copies, 'dp', 0, 0)]
    all_to_all x0 -> x1, starting transfers between devices: none -> 8.32 us  [on_device(): power_pieces = lax.all_to_all(copies, 'dp', 0, 0)]
    pallas_call x13 -> x14, Pallas kernels: 51.1 us -> 56.1 us  [kernel_call(): pl.pallas_call(call, grid=(grid,), in_specs=[whole(a) if s is None else s...]
    all_to_all x0 -> x1, waiting for transfers between devices: none -> 4.48 us  [on_device(): power_pieces = lax.all_to_all(copies, 'dp', 0, 0)]
    unnamed x18 -> x20, local copies, waits for them, and re-layouts: 14.8 us -> 16.9 us
  transfers between devices with their start and end apart: 17 -> 18, of which waited for: 14 -> 14; matrix products, arithmetic and copies ran while one was open for 0% -> 0% of each run, Pallas kernels for 17% -> 21%
where the time goes in v5:
time: 163 us; the launch traced here: 162 us
  Pallas kernels  56.1 us (34%)
  starting transfers between devices  45.7 us (28%)
  waiting for transfers between devices  29.6 us (18%)
  local copies, waits for them, and re-layouts  16.9 us (10%)
  between operations  14.2 us (9%)
    pallas_call x14, Pallas kernels, kernel_call(): pl.pallas_call(call, grid=(grid,), in_specs=[whole(a) if s is None else s...  56.1 us
    unnamed x20, local copies, waits for them, and re-layouts  16.9 us
    ppermute x13, starting transfers between devices, fetch(): return lax.ppermute(array, AXES, receive_from(**offsets))  15.4 us
    ppermute x13, waiting for transfers between devices, fetch(): return lax.ppermute(array, AXES, receive_from(**offsets))  14.4 us
    all_to_all x1, waiting for transfers between devices, on_device(): terms = lax.all_to_all(terms, 'dp', 0, 0)  9.48 us
    all_to_all x1, starting transfers between devices, on_device(): hq = lax.all_to_all(hq, 'tensor', 0, 0)  8.6 us
    all_to_all x1, starting transfers between devices, on_device(): power_pieces = lax.all_to_all(copies, 'dp', 0, 0)  8.32 us
    all_to_all x1, starting transfers between devices, on_device(): terms = lax.all_to_all(terms, 'dp', 0, 0)  7.2 us
  transfers between devices with their start and end apart: 18, of which 14 were waited for; matrix products, arithmetic and copies ran while one was open for 0% of the time, Pallas kernels for 21%

profile of v5, /device:TPU:1, one launch (start us, length us, event | category | flops | bytes accessed | tf_op | source)
XLA Modules:
  0.0 162.4 jit_solution(16797757788438837182)
XLA Ops:
  7.2 0.0 copy-start.5
  7.2 0.0 all-gather.2.cloned.1.call-start
  7.2 0.7 all-gather.2.cloned.1.call-update
  7.9 0.0 copy-start.2
  7.9 2.0 %copy-done.2 = bf16[2048,896]{1,0:T(8,128)(2,1)S(1)} copy-done((bf16[2048,896]{1,0:T(8,128)(2,1)S(1)}, bf16[2048,896]{1,0:T(8,128)(2,1)}, u32[]{:S(2)}) %copy-start.2) | copy-done | bytes 3670040
  9.9 0.0 copy-start.7
  10.0 0.9 copy-done.7
  10.8 2.5 %shard_map.59 = f32[16,32,128]{2,1,0:T(8,128)} custom-call(f32[32,896]{1,0:T(8,128)S(1)} %bitcast.8, bf16[2048,896]{1,0:T(8,128)(2,1)S(1)} %copy-done.2), custom_call_target="tpu_custom_call" | custom-call | flops 1048576 | bytes 65536 | tf_op jit(solution)/shard_map/pallas_call | solution.py:59
  13.4 8.6 %all-to-all-start = ((f32[16,32,128]{2,1,0:T(8,128)}), f32[16,32,128]{2,1,0:T(8,128)S(1)}, u32[]{:S(2)}, u32[]{:S(2)}) async-start(f32[16,32,128]{2,1,0:T(8,128)} %shard_map.59), calls=%async_computation | async-start | bytes 524288 | tf_op jit(solution)/shard_map/all_to_all | solution.py:265
  22.0 0.0 copy-start
  22.0 3.8 %copy-done = bf16[1,4096,896]{2,1,0:T(8,128)(2,1)S(1)} copy-done((bf16[1,4096,896]{2,1,0:T(8,128)(2,1)S(1)}, bf16[1,4096,896]{2,1,0:T(8,128)(2,1)}, u32[]{:S(2)}) %copy-start) | copy-done | bytes 7340056
  25.8 0.0 copy-start.8
  25.8 0.9 copy-done.8
  26.7 3.4 %shard_map.60.refs_2_ = f32[32,4096]{1,0:T(8,128)S(1)} custom-call(f32[32,896]{1,0:T(8,128)S(1)} %bitcast.9, bf16[4096,896]{1,0:T(8,128)(2,1)S(1)} %bitcast.6), custom_call_target="tpu_custom_call" | custom-call | flops 1048576 | bytes 65536 | tf_op jit(solution)/shard_map/pallas_call | solution.py:59
  30.1 0.0 all-to-all-done.refs_0_
  30.1 0.0 copy-done.5
  30.1 1.4 shard_map.61
  31.5 7.2 %all-to-all-start.1 = ((f32[8,32,512]{2,1,0:T(8,128)}), f32[8,32,512]{2,1,0:T(8,128)S(1)}, u32[]{:S(2)}, u32[]{:S(2)}) async-start(f32[8,32,512]{2,1,0:T(8,128)} %shard_map.61), calls=%async_computation.1 | async-start | bytes 1048576 | tf_op jit(solution)/shard_map/all_to_all | solution.py:283
  38.7 9.5 %all-to-all-done.1.refs_1_ = f32[8,32,512]{2,1,0:T(8,128)S(1)} async-done(((f32[8,32,512]{2,1,0:T(8,128)}), f32[8,32,512]{2,1,0:T(8,128)S(1)}, u32[]{:S(2)}, u32[]{:S(2)}) %all-to-all-start.1) | async-done | bytes 524320 | tf_op jit(solution)/shard_map/all_to_all | solution.py:283
  48.2 1.1 collective-permute-start
  49.3 0.6 collective-permute-start.1
  49.8 0.6 collective-permute-start.2
  50.4 0.5 collective-permute-done.refs_1_
  50.9 2.5 %collective-permute-done.1.refs_2_ = f32[32,128]{1,0:T(8,128)S(1)} collective-permute-done((f32[32,128]{1,0:T(8,128)S(1)}, f32[32,128]{1,0:T(8,128)S(1)}, u32[]{:S(2)}, u32[]{:S(2)}) %collective-permute-start.1) | collective-permute-done | bytes 16416 | tf_op jit(solution)/shard_map/ppermute | solution.py:31
  53.4 0.3 collective-permute-done.2.refs_3_
  53.6 1.2 collective-permute-start.5
  54.8 2.4 %collective-permute-start.4 = (f32[32,128]{1,0:T(8,128)S(1)}, f32[32,128]{1,0:T(8,128)S(1)}, u32[]{:S(2)}, u32[]{:S(2)}) collective-permute-start(f32[32,128]{1,0:T(8,128)S(1)} %shard_map.63.refs_0_), channel_id=1, source_target_pairs={{8,0},{9,1},{10,2},{11,3},{12,4},{13,5},{14,6},{15,7},{0,8},{1,9},... | collective-permute-start | bytes 49160 | tf_op jit(solution)/shard_map/ppermute | solution.py:31
  57.2 1.2 collective-permute-start.3
  58.4 0.0 collective-permute-done.5.refs_3_
  58.4 0.7 collective-permute-done.4.refs_2_
  59.1 1.4 collective-permute-done.3.refs_1_
  60.5 0.0 collective-permute-start.8
  60.5 1.6 collective-permute-start.7
  62.1 1.7 %collective-permute-start.6 = (f32[32,128]{1,0:T(8,128)S(1)}, f32[32,128]{1,0:T(8,128)S(1)}, u32[]{:S(2)}, u32[]{:S(2)}) collective-permute-start(f32[32,128]{1,0:T(8,128)S(1)} %shard_map.64.refs_1_), channel_id=1, source_target_pairs={{1,0},{2,1},{3,2},{0,3},{5,4},{6,5},{7,6},{4,7},{9,8},{10,9},{11,1... | collective-permute-start | bytes 49160 | tf_op jit(solution)/shard_map/ppermute | solution.py:31
  63.8 1.3 collective-permute-done.8.refs_4_
  65.1 0.0 collective-permute-done.7.refs_3_
  65.1 1.0 collective-permute-done.6.refs_2_
  66.1 0.8 shard_map.65.refs_1_
  67.0 8.3 %all-to-all-start.2 = ((f32[8,4,32,128]{3,2,1,0:T(8,128)}), f32[8,4,32,128]{3,2,1,0:T(8,128)S(1)}, u32[]{:S(2)}, u32[]{:S(2)}) async-start(f32[8,4,32,128]{3,2,1,0:T(8,128)} %shard_map.65.refs_1_), calls=%async_computation.2 | async-start | bytes 1048576 | tf_op jit(solution)/shard_map/all_to_all | solution.py:299
  75.3 5.0 %shard_map.66.refs_2_.refs_1_ = bf16[896,2048]{1,0:T(8,128)(2,1)} custom-call(bf16[2048,896]{1,0:T(8,128)(2,1)} %refs_1_.7, f32[8,4,32,128]{3,2,1,0:T(8,128)} %shard_map.65.refs_1_), custom_call_target="tpu_custom_call" | custom-call | flops 1048576 | bytes 65536 | tf_op jit(solution)/shard_map/pallas_call | solution.py:59
  80.3 4.5 %all-to-all-done.2.refs_0_ = f32[8,4,32,128]{3,2,1,0:T(8,128)S(1)} async-done(((f32[8,4,32,128]{3,2,1,0:T(8,128)}), f32[8,4,32,128]{3,2,1,0:T(8,128)S(1)}, u32[]{:S(2)}, u32[]{:S(2)}) %all-to-all-start.2) | async-done | bytes 524320 | tf_op jit(solution)/shard_map/all_to_all | solution.py:299
  84.8 2.0 %copy-done.4 = bf16[896,2048]{1,0:T(8,128)(2,1)S(1)} copy-done((bf16[896,2048]{1,0:T(8,128)(2,1)S(1)}, bf16[896,2048]{1,0:T(8,128)(2,1)}, u32[]{:S(2)}) %copy-start.4) | copy-done | bytes 3670040
  86.8 1.5 shard_map.67
  88.4 6.1 %all-to-all-start.3 = ((f32[16,32,128]{2,1,0:T(8,128)}), f32[16,32,128]{2,1,0:T(8,128)S(1)}, u32[]{:S(2)}, u32[]{:S(2)}) async-start(f32[16,32,128]{2,1,0:T(8,128)} %get-tuple-element.22), calls=%async_computation.3 | async-start | bytes 524288 | tf_op jit(solution)/shard_map/all_to_all | solution.py:307
  94.5 0.0 copy-start.1
  94.5 3.1 %copy-done.1 = bf16[1,4096,896]{2,1,0:T(8,128)(2,1)S(1)} copy-done((bf16[1,4096,896]{2,1,0:T(8,128)(2,1)S(1)}, bf16[1,4096,896]{2,1,0:T(8,128)(2,1)}, u32[]{:S(2)}) %copy-start.1) | copy-done | bytes 7340056
  97.6 6.4 %shard_map.68 = (f32[32,896]{1,0:T(8,128)S(1)}, f32[32,32]{1,0:T(8,128)S(1)}, bf16[192,4096]{1,0:T(8,128)(2,1)S(1)}) custom-call(f32[32,4096]{1,0:T(8,128)S(1)} %get-tuple-element.18.refs_0_, bf16[96,4096]{1,0:T(8,128)(2,1)S(1)} %get-tuple-element.19.refs_1_, bf16[4096,896]{1,0:T(8,128)(2,1)S(1)} %bitcast.7), custom_call_target="tpu_custom_call" | custom-call | flops 1048576 | bytes 65536 | tf_op jit(solution)/shard_map/pallas_call | solution.py:59
  104.0 0.0 copy-start.6
  104.0 1.1 copy-done.6
  105.2 0.5 all-to-all-done.3.refs_0_
  105.7 2.1 %copy-done.3 = bf16[2048,896]{1,0:T(8,128)(2,1)S(1)} copy-done((bf16[2048,896]{1,0:T(8,128)(2,1)S(1)}, bf16[2048,896]{1,0:T(8,128)(2,1)}, u32[]{:S(2)}) %copy-start.3) | copy-done | bytes 3670040
  107.8 1.2 shard_map.69
  109.1 2.4 %collective-permute-start.9 = (f32[32,896]{1,0:T(8,128)S(1)}, f32[32,896]{1,0:T(8,128)S(1)}, u32[]{:S(2)}, u32[]{:S(2)}) collective-permute-start(f32[32,896]{1,0:T(8,128)S(1)} %shard_map.69), channel_id=1, source_target_pairs={{16,0},{17,1},{18,2},{19,3},{20,4},{21,5},{22,6},{23,7},{24,8},{25... | collective-permute-start | bytes 344072 | tf_op jit(solution)/shard_map/ppermute | solution.py:31
  111.5 1.0 collective-permute-done.9
  112.5 0.3 collective-permute-start.12
  112.8 1.6 collective-permute-start.11
  114.4 0.9 collective-permute-start.10
  115.3 3.7 %collective-permute-done.12.refs_4_ = f32[32,896]{1,0:T(8,128)S(1)} collective-permute-done((f32[32,896]{1,0:T(8,128)S(1)}, f32[32,896]{1,0:T(8,128)S(1)}, u32[]{:S(2)}, u32[]{:S(2)}) %collective-permute-start.12) | collective-permute-done | bytes 114720 | tf_op jit(solution)/shard_map/ppermute | solution.py:31
  119.0 0.7 collective-permute-done.11.refs_3_
  119.7 1.3 collective-permute-done.10.refs_2_
  121.0 0.9 shard_map.70
  121.9 0.8 copy-done.9
  122.7 10.1 %shard_map.71.refs_2_ = f32[4096,896]{1,0:T(8,128)} custom-call(bf16[192,4096]{1,0:T(8,128)(2,1)} %copy-done.6, bf16[192,896]{1,0:T(8,128)(2,1)} %copy-done.9, bf16[4096,896]{1,0:T(8,128)(2,1)} %bitcast.5), custom_call_target="tpu_custom_call" | custom-call | flops 1048576 | bytes 65536 | tf_op jit(solution)/shard_map/pallas_call | solution.py:59
  132.8 22.7 %shard_map.72 = bf16[4096,896]{1,0:T(8,128)(2,1)} custom-call(bf16[2048,4096]{1,0:T(8,128)(2,1)} %all-gather.2.cloned.1.call-done.refs_0_, bf16[896,2048]{1,0:T(8,128)(2,1)} %shard_map.66.refs_2_.refs_1_, f32[4096,896]{1,0:T(8,128)} %shard_map.71.refs_2_), custom_call_target="tpu_custom_call" | custom-call | flops 1048576 | bytes 65536 | tf_op jit(solution)/shard_map/pallas_call | solution.py:59
  (8 shorter events, 0.1 us)
Async XLA Ops:
  7.2 22.9 %copy-start.5 = (bf16[128,4096]{1,0:T(8,128)(2,1)S(1)}, bf16[128,4096]{1,0:T(8,128)(2,1)}, u32[]{:S(2)}) copy-start(bf16[128,4096]{1,0:T(8,128)(2,1)} %refs_1_.6) | copy-start | bytes 3145732
  7.2 125.6 %all-gather.2.cloned.1.call-start = ((), (), s32[]{:S(2)}) async-start(), calls=%async_computation.4 | async-start | bytes 17825792 | tf_op jit(solution)/shard_map/all_gather | solution.py:257
  7.9 2.0 %copy-start.2 = (bf16[2048,896]{1,0:T(8,128)(2,1)S(1)}, bf16[2048,896]{1,0:T(8,128)(2,1)}, u32[]{:S(2)}) copy-start(bf16[2048,896]{1,0:T(8,128)(2,1)} %refs_1_.7) | copy-start | bytes 11010052
  9.9 0.9 copy-start.7
  13.4 16.7 %all-to-all-start = ((f32[16,32,128]{2,1,0:T(8,128)}), f32[16,32,128]{2,1,0:T(8,128)S(1)}, u32[]{:S(2)}, u32[]{:S(2)}) async-start(f32[16,32,128]{2,1,0:T(8,128)} %shard_map.59), calls=%async_computation | async-start | bytes 524288 | tf_op jit(solution)/shard_map/all_to_all | solution.py:265
  22.0 3.8 %copy-start = (bf16[1,4096,896]{2,1,0:T(8,128)(2,1)S(1)}, bf16[1,4096,896]{2,1,0:T(8,128)(2,1)}, u32[]{:S(2)}) copy-start(bf16[1,4096,896]{2,1,0:T(8,128)(2,1)} %param.6) | copy-start | bytes 22020100
  25.8 0.9 copy-start.8
  31.5 16.7 %all-to-all-start.1 = ((f32[8,32,512]{2,1,0:T(8,128)}), f32[8,32,512]{2,1,0:T(8,128)S(1)}, u32[]{:S(2)}, u32[]{:S(2)}) async-start(f32[8,32,512]{2,1,0:T(8,128)} %shard_map.61), calls=%async_computation.1 | async-start | bytes 1048576 | tf_op jit(solution)/shard_map/all_to_all | solution.py:283
  48.2 2.7 %collective-permute-start = (f32[32,128]{1,0:T(8,128)S(1)}, f32[32,128]{1,0:T(8,128)S(1)}, u32[]{:S(2)}, u32[]{:S(2)}) collective-permute-start(f32[32,128]{1,0:T(8,128)S(1)} %get-tuple-element.15), channel_id=1, source_target_pairs={{1,0},{2,1},{3,2},{0,3},{5,4},{6,5},{7,6},{4,7},{9,8},{10,9},{11,1... | collective-permute-start | bytes 49160 | tf_op jit(solution)/shard_map/ppermute | solution.py:31
  49.3 4.1 %collective-permute-start.1 = (f32[32,128]{1,0:T(8,128)S(1)}, f32[32,128]{1,0:T(8,128)S(1)}, u32[]{:S(2)}, u32[]{:S(2)}) collective-permute-start(f32[32,128]{1,0:T(8,128)S(1)} %get-tuple-element.16), channel_id=1, source_target_pairs={{2,0},{3,1},{0,2},{1,3},{6,4},{7,5},{4,6},{5,7},{10,8},{11,9},{8,1... | collective-permute-start | bytes 49160 | tf_op jit(solution)/shard_map/ppermute | solution.py:31
  49.8 3.8 %collective-permute-start.2 = (f32[32,128]{1,0:T(8,128)S(1)}, f32[32,128]{1,0:T(8,128)S(1)}, u32[]{:S(2)}, u32[]{:S(2)}) collective-permute-start(f32[32,128]{1,0:T(8,128)S(1)} %get-tuple-element.17), channel_id=1, source_target_pairs={{3,0},{0,1},{1,2},{2,3},{7,4},{4,5},{5,6},{6,7},{11,8},{8,9},{9,10... | collective-permute-start | bytes 49160 | tf_op jit(solution)/shard_map/ppermute | solution.py:31
  53.6 4.8 %collective-permute-start.5 = (f32[32,128]{1,0:T(8,128)S(1)}, f32[32,128]{1,0:T(8,128)S(1)}, u32[]{:S(2)}, u32[]{:S(2)}) collective-permute-start(f32[32,128]{1,0:T(8,128)S(1)} %shard_map.63.refs_0_), channel_id=1, source_target_pairs={{12,0},{13,1},{14,2},{15,3},{0,4},{1,5},{2,6},{3,7},{4,8},{5,9},{6... | collective-permute-start | bytes 49160 | tf_op jit(solution)/shard_map/ppermute | solution.py:31
  54.8 4.2 %collective-permute-start.4 = (f32[32,128]{1,0:T(8,128)S(1)}, f32[32,128]{1,0:T(8,128)S(1)}, u32[]{:S(2)}, u32[]{:S(2)}) collective-permute-start(f32[32,128]{1,0:T(8,128)S(1)} %shard_map.63.refs_0_), channel_id=1, source_target_pairs={{8,0},{9,1},{10,2},{11,3},{12,4},{13,5},{14,6},{15,7},{0,8},{1,9},... | collective-permute-start | bytes 49160 | tf_op jit(solution)/shard_map/ppermute | solution.py:31
  57.2 3.3 %collective-permute-start.3 = (f32[32,128]{1,0:T(8,128)S(1)}, f32[32,128]{1,0:T(8,128)S(1)}, u32[]{:S(2)}, u32[]{:S(2)}) collective-permute-start(f32[32,128]{1,0:T(8,128)S(1)} %shard_map.63.refs_0_), channel_id=1, source_target_pairs={{4,0},{5,1},{6,2},{7,3},{8,4},{9,5},{10,6},{11,7},{12,8},{13,9},{1... | collective-permute-start | bytes 49160 | tf_op jit(solution)/shard_map/ppermute | solution.py:31
  60.5 4.6 %collective-permute-start.8 = (f32[32,128]{1,0:T(8,128)S(1)}, f32[32,128]{1,0:T(8,128)S(1)}, u32[]{:S(2)}, u32[]{:S(2)}) collective-permute-start(f32[32,128]{1,0:T(8,128)S(1)} %shard_map.64.refs_1_), channel_id=1, source_target_pairs={{3,0},{0,1},{1,2},{2,3},{7,4},{4,5},{5,6},{6,7},{11,8},{8,9},{9,10... | collective-permute-start | bytes 49160 | tf_op jit(solution)/shard_map/ppermute | solution.py:31
  60.5 4.6 %collective-permute-start.7 = (f32[32,128]{1,0:T(8,128)S(1)}, f32[32,128]{1,0:T(8,128)S(1)}, u32[]{:S(2)}, u32[]{:S(2)}) collective-permute-start(f32[32,128]{1,0:T(8,128)S(1)} %shard_map.64.refs_1_), channel_id=1, source_target_pairs={{2,0},{3,1},{0,2},{1,3},{6,4},{7,5},{4,6},{5,7},{10,8},{11,9},{8,1... | collective-permute-start | bytes 49160 | tf_op jit(solution)/shard_map/ppermute | solution.py:31
  62.1 4.1 %collective-permute-start.6 = (f32[32,128]{1,0:T(8,128)S(1)}, f32[32,128]{1,0:T(8,128)S(1)}, u32[]{:S(2)}, u32[]{:S(2)}) collective-permute-start(f32[32,128]{1,0:T(8,128)S(1)} %shard_map.64.refs_1_), channel_id=1, source_target_pairs={{1,0},{2,1},{3,2},{0,3},{5,4},{6,5},{7,6},{4,7},{9,8},{10,9},{11,1... | collective-permute-start | bytes 49160 | tf_op jit(solution)/shard_map/ppermute | solution.py:31
  67.0 17.8 %all-to-all-start.2 = ((f32[8,4,32,128]{3,2,1,0:T(8,128)}), f32[8,4,32,128]{3,2,1,0:T(8,128)S(1)}, u32[]{:S(2)}, u32[]{:S(2)}) async-start(f32[8,4,32,128]{3,2,1,0:T(8,128)} %shard_map.65.refs_1_), calls=%async_computation.2 | async-start | bytes 1048576 | tf_op jit(solution)/shard_map/all_to_all | solution.py:299
  84.8 2.0 %copy-start.4 = (bf16[896,2048]{1,0:T(8,128)(2,1)S(1)}, bf16[896,2048]{1,0:T(8,128)(2,1)}, u32[]{:S(2)}) copy-start(bf16[896,2048]{1,0:T(8,128)(2,1)} %shard_map.66.refs_2_.refs_1_) | copy-start | bytes 11010052
  88.4 17.3 %all-to-all-start.3 = ((f32[16,32,128]{2,1,0:T(8,128)}), f32[16,32,128]{2,1,0:T(8,128)S(1)}, u32[]{:S(2)}, u32[]{:S(2)}) async-start(f32[16,32,128]{2,1,0:T(8,128)} %get-tuple-element.22), calls=%async_computation.3 | async-start | bytes 524288 | tf_op jit(solution)/shard_map/all_to_all | solution.py:307
  94.5 3.2 %copy-start.1 = (bf16[1,4096,896]{2,1,0:T(8,128)(2,1)S(1)}, bf16[1,4096,896]{2,1,0:T(8,128)(2,1)}, u32[]{:S(2)}) copy-start(bf16[1,4096,896]{2,1,0:T(8,128)(2,1)} %param.6) | copy-start | bytes 22020100
  104.0 1.1 copy-start.6
  105.7 2.1 %copy-start.3 = (bf16[2048,896]{1,0:T(8,128)(2,1)S(1)}, bf16[2048,896]{1,0:T(8,128)(2,1)}, u32[]{:S(2)}) copy-start(bf16[2048,896]{1,0:T(8,128)(2,1)} %refs_1_.7) | copy-start | bytes 11010052
  109.1 3.4 %collective-permute-start.9 = (f32[32,896]{1,0:T(8,128)S(1)}, f32[32,896]{1,0:T(8,128)S(1)}, u32[]{:S(2)}, u32[]{:S(2)}) collective-permute-start(f32[32,896]{1,0:T(8,128)S(1)} %shard_map.69), channel_id=1, source_target_pairs={{16,0},{17,1},{18,2},{19,3},{20,4},{21,5},{22,6},{23,7},{24,8},{25... | collective-permute-start | bytes 344072 | tf_op jit(solution)/shard_map/ppermute | solution.py:31
  112.5 6.6 %collective-permute-start.12 = (f32[32,896]{1,0:T(8,128)S(1)}, f32[32,896]{1,0:T(8,128)S(1)}, u32[]{:S(2)}, u32[]{:S(2)}) collective-permute-start(f32[32,896]{1,0:T(8,128)S(1)} %add.8.refs_1_), channel_id=1, source_target_pairs={{96,0},{97,1},{98,2},{99,3},{100,4},{101,5},{102,6},{103,7},{104,8... | collective-permute-start | bytes 344072 | tf_op jit(solution)/shard_map/ppermute | solution.py:31
  112.8 6.9 %collective-permute-start.11 = (f32[32,896]{1,0:T(8,128)S(1)}, f32[32,896]{1,0:T(8,128)S(1)}, u32[]{:S(2)}, u32[]{:S(2)}) collective-permute-start(f32[32,896]{1,0:T(8,128)S(1)} %add.8.refs_1_), channel_id=1, source_target_pairs={{64,0},{65,1},{66,2},{67,3},{68,4},{69,5},{70,6},{71,7},{72,8},{73... | collective-permute-start | bytes 344072 | tf_op jit(solution)/shard_map/ppermute | solution.py:31
  114.4 6.7 %collective-permute-start.10 = (f32[32,896]{1,0:T(8,128)S(1)}, f32[32,896]{1,0:T(8,128)S(1)}, u32[]{:S(2)}, u32[]{:S(2)}) collective-permute-start(f32[32,896]{1,0:T(8,128)S(1)} %add.8.refs_1_), channel_id=1, source_target_pairs={{32,0},{33,1},{34,2},{35,3},{36,4},{37,5},{38,6},{39,7},{40,8},{41... | collective-permute-start | bytes 344072 | tf_op jit(solution)/shard_map/ppermute | solution.py:31
  121.9 0.8 copy-start.9
Sparse Core Ops, SparseCore 0:
  10.1 118.5 all-gather.1
